TPU v7x, 128 devices: a whole 4x4x4 slice. The times are simulated.
128 devices in a mesh: pair: 4 (over z), node: 32 (over x, y, core).
Axes of the slice: x: 4, y: 4, z: 4, core: 2. Of those that a mesh axis runs over, the one named last changes fastest.
Arguments:
- node_feats: bfloat16 [4096, 1024], P('node'), may hold values from -6 to 6
- msg_weight: bfloat16 [1024, 1024], replicated, may hold values from -0.1875 to 0.1875
- msg_bias: float32 [1024], replicated, may hold values from -3 to 3
- edge_source: int32 [8192], P('node'), may hold values from 0 to 127
- edge_slot: int32 [8192], P('node'), may hold values from 0 to 511, as said below
- edge_target: int32 [8192], P('node'), may hold values from 0 to 127
- edge_weight: bfloat16 [8192], P('node'), may hold values from 0.25 to 4
- update_weight: bfloat16 [2048, 1024], replicated, may hold values from -0.125 to 0.125
- update_bias: float32 [1024], replicated, may hold values from -3 to 3
- pair_ids: int32 [8192, 2], P(('pair', 'node')), may hold values from 0 to 4095, as said below
- neg_ids: int32 [8192, 15], P(('pair', 'node')), may hold values from 0 to 4095, as said below
- hidden_weight: bfloat16 [3072, 1024], replicated, may hold values from -0.109375 to 0.109375
- hidden_bias: float32 [1024], replicated, may hold values from -3 to 3
- score_weight: bfloat16 [1024], replicated, may hold values from -0.1875 to 0.1875
- score_grad: float32 [8192, 16], P(('pair', 'node')), may hold values from -0.625 to 0.625
Outputs:
- embedding: bfloat16 [4096, 1024], P('node')
- scores: float32 [8192, 16], P(('pair', 'node'))
- grad_hidden_weight: float32 [3072, 1024], P(('pair', 'node'))
- grad_hidden_bias: float32 [1024], P(('pair', 'node'))
- grad_score_weight: float32 [1024], P(('pair', 'node'))
Inputs may be any that keep to these rules, and one draw needn't show every extreme that they name: `edge_slot`: the 256 edges of one index of node (aligned blocks) take distinct slots; slot // 16 names the owner of the edge's destination, so one device sends at most 16 edges to one owner, and some owner receives exactly 16 from every device. Global node ids. Among the ids of pair_ids and neg_ids of one device's 64 pairs (aligned blocks) at most 68 fall in one owner's range of 128 ids (id // 128), and exactly 68 for some owner on every device. `neg_ids`: global node ids, with the bound stated for pair_ids on the same pairs.
All inputs are finite; a program needn't handle non-finite values.
Results may differ from a plain program's by a relative error of at most 0.025.
Values may be sent and summed in bfloat16 or wider, within the bound.
A program may use at most 128 MiB of HBM per device.

v0:
```python
import jax
import jax.numpy as jnp
from jax import lax
from jax.sharding import PartitionSpec as P


def score_pairs(fetched, pairs_dev, hidden_weight, hidden_bias, score_weight, score_cot):
    feature_dim = fetched.shape[1]
    query = fetched[: 2 * pairs_dev].reshape(pairs_dev, 2, feature_dim)
    negatives = fetched[2 * pairs_dev :].reshape(pairs_dev, -1, feature_dim)
    cand_rows = jnp.concatenate([query[:, 1:2, :], negatives], axis=1)
    query_full = jnp.broadcast_to(query[:, 0:1, :], cand_rows.shape)
    product = (query_full.astype(jnp.float32) * cand_rows.astype(jnp.float32)).astype(jnp.bfloat16)
    inputs = jnp.concatenate([query_full, cand_rows, product], axis=-1).reshape(-1, 3 * feature_dim)
    pre_act = jnp.dot(inputs, hidden_weight, preferred_element_type=jnp.float32) + hidden_bias
    sigmoid_pre = jax.nn.sigmoid(pre_act)
    hidden = (pre_act * sigmoid_pre).astype(jnp.bfloat16)
    scores = jnp.dot(hidden, score_weight, preferred_element_type=jnp.float32)
    cot_flat = score_cot.reshape(-1)
    grad_score = jnp.sum(cot_flat[:, None] * hidden.astype(jnp.float32), axis=0)
    hidden_grad = cot_flat[:, None] * score_weight.astype(jnp.float32)[None, :]
    pre_grad = (hidden_grad * sigmoid_pre * (1.0 + pre_act * (1.0 - sigmoid_pre))).astype(
        jnp.bfloat16
    )
    grad_bias = jnp.sum(pre_grad.astype(jnp.float32), axis=0)
    grad_weight = lax.dot_general(
        inputs, pre_grad, (((0,), (0,)), ((), ())), preferred_element_type=jnp.float32
    )
    return (scores.reshape(pairs_dev, -1), grad_weight, grad_bias, grad_score)


def body(
    node_feats,
    msg_weight,
    msg_bias,
    edge_source,
    edge_slot,
    edge_target,
    edge_weight,
    update_weight,
    update_bias,
    pair_ids,
    neg_ids,
    hidden_weight,
    hidden_bias,
    score_weight,
    score_grad,
):
    node_count = lax.axis_size("node")
    node_dev, feature_dim = node_feats.shape
    edges_dev = edge_source.shape[0]
    slot_count = max(2, 2 * edges_dev // node_count)
    project = jax.nn.relu(
        jnp.dot(node_feats, msg_weight, preferred_element_type=jnp.float32) + msg_bias
    )
    weight_f = edge_weight.astype(jnp.float32)
    message = (weight_f[:, None] * project[edge_source]).astype(jnp.bfloat16)
    slot_total = node_count * slot_count
    buffer = jnp.zeros((slot_total, feature_dim), jnp.bfloat16).at[edge_slot].set(message)
    weight_slots = jnp.zeros((slot_total,), jnp.bfloat16).at[edge_slot].set(edge_weight)
    target_slots = jnp.zeros((slot_total,), jnp.int32).at[edge_slot].set(edge_target)
    got_rows, got_weights, got_targets = (
        lax.all_to_all(
            buffer.reshape(node_count, slot_count, feature_dim),
            "node",
            split_axis=0,
            concat_axis=0,
            tiled=True,
        ),
        lax.all_to_all(
            weight_slots.reshape(node_count, slot_count),
            "node",
            split_axis=0,
            concat_axis=0,
            tiled=True,
        ),
        lax.all_to_all(
            target_slots.reshape(node_count, slot_count),
            "node",
            split_axis=0,
            concat_axis=0,
            tiled=True,
        ),
    )
    onehot = (
        got_targets.reshape(-1)[None, :] == jnp.arange(node_dev, dtype=jnp.int32)[:, None]
    ).astype(jnp.bfloat16)
    sums = jnp.dot(onehot, got_rows.reshape(-1, feature_dim), preferred_element_type=jnp.float32)
    totals = jnp.dot(onehot, got_weights.reshape(-1), preferred_element_type=jnp.float32)
    average = (sums / jnp.maximum(totals, 1.0)[:, None]).astype(jnp.bfloat16)
    joined = jnp.concatenate([node_feats, average], axis=1)
    rectified = jax.nn.relu(
        jnp.dot(joined, update_weight, preferred_element_type=jnp.float32) + update_bias
    )
    embedding = (
        rectified * lax.rsqrt(jnp.mean(rectified * rectified, axis=-1, keepdims=True) + 1e-06)
    ).astype(jnp.bfloat16)
    pairs_dev = pair_ids.shape[0]
    ask_ids = jnp.concatenate([pair_ids.reshape(-1), neg_ids.reshape(-1)])
    shard_rows = lax.all_gather(embedding, "node", axis=0, tiled=True)
    onehot = (ask_ids[:, None] == jnp.arange(shard_rows.shape[0], dtype=jnp.int32)[None, :]).astype(
        jnp.bfloat16
    )
    gathered = jnp.dot(onehot, shard_rows, preferred_element_type=jnp.float32)
    fetched = gathered.astype(jnp.bfloat16)
    scores, grad_weight, grad_bias, grad_score = score_pairs(
        fetched, pairs_dev, hidden_weight, hidden_bias, score_weight, score_grad
    )
    shared_weight, shared_bias, shared_score = (
        lax.psum_scatter(grad_weight, ("pair", "node"), scatter_dimension=0, tiled=True),
        lax.psum_scatter(grad_bias, ("pair", "node"), scatter_dimension=0, tiled=True),
        lax.psum_scatter(grad_score, ("pair", "node"), scatter_dimension=0, tiled=True),
    )
    return (embedding, scores, shared_weight, shared_bias, shared_score)


def solution(mesh):
    return jax.shard_map(
        body,
        mesh=mesh,
        in_specs=(
            P("node", None),
            P(),
            P(),
            P("node"),
            P("node"),
            P("node"),
            P("node"),
            P(),
            P(),
            P(("pair", "node"), None),
            P(("pair", "node"), None),
            P(),
            P(),
            P(),
            P(("pair", "node"), None),
        ),
        out_specs=(
            P("node", None),
            P(("pair", "node"), None),
            P(("pair", "node"), None),
            P(("pair", "node")),
            P(("pair", "node")),
        ),
        check_vma=False,
    )
```

profile of v0, /device:TPU:1, one launch (start us, length us, event | category | flops | bytes accessed | tf_op | source)
XLA Modules:
  0.0 387.7 jit_solution(5888716974621339321)
XLA Ops:
  7.2 0.0 copy-start
  7.2 0.8 compare_select_fusion.1
  8.0 2.3 scatter_custom_fusion.2
  10.3 0.7 all_to_all.20
  11.0 8.6 %all-to-all-start.2 = ((bf16[32,1,16]{2,1,0:T(2,128)(2,1)}), bf16[32,1,16]{2,1,0:T(2,128)(2,1)S(1)}, u32[]{:S(2)}, u32[]{:S(2)}) async-start(bf16[32,1,16]{2,1,0:T(2,128)(2,1)} %all_to_all.20), calls=%async_computation.2 | async-start | bytes 32768 | tf_op jit(solution)/shard_map/all_to_all | solution.py:70
  19.6 0.0 copy-done
  19.6 0.0 copy-start.1
  19.6 0.0 copy-start.5
  19.6 1.4 fusion.7
  21.1 0.7 compare_select_fusion
  21.8 1.6 scatter_custom_fusion
  23.3 0.7 all_to_all.15
  24.0 2.4 all-to-all-done.2
  26.5 4.9 %all-to-all-start = ((s32[32,1,16]{2,1,0:T(1,128)}), s32[32,1,16]{2,1,0:T(1,128)S(1)}, u32[]{:S(2)}, u32[]{:S(2)}) async-start(s32[32,1,16]{2,1,0:T(1,128)} %bitcast), calls=%async_computation | async-start | bytes 32768 | tf_op jit(solution)/shard_map/all_to_all | solution.py:77
  31.4 0.7 convert_element_type.44
  32.1 3.9 %scatter_custom_fusion.1 = bf16[512,1024]{1,0:T(8,128)(2,1)} fusion(s32[256]{0:T(256)S(1)} %compare_select_fusion.1, f32[256]{0:T(256)S(1)} %convert_element_type.44, bf16[]{:T(256)} %constant.10.clone.1, f32[128,1024]{1,0:T(8,128)S(1)} %fusion.7, s32[1024]{0:T(1024)S(1)} %pad_clamp_fusion), kind=kCustom, calls=%fused_computation.28 | custom fusion | flops 524288 | bytes 1577986 | tf_op jit(solution)/shard_map/scatter | solution.py:59
  36.0 2.3 all-to-all-done
  38.3 5.1 %all-to-all-start.1 = ((bf16[32,16,1024]{2,1,0:T(8,128)(2,1)}), bf16[32,16,1024]{2,1,0:T(8,128)(2,1)S(1)}, u32[]{:S(2)}, u32[]{:S(2)}) async-start(bf16[32,16,1024]{2,1,0:T(8,128)(2,1)} %bitcast.1), calls=%async_computation.1 | async-start | bytes 2097152 | tf_op jit(solution)/shard_map/all_to_all | solution.py:63
  43.4 0.0 all-gather.2.cloned.1.call-start
  43.4 0.1 reduce.1
  43.5 0.1 reshape.111
  43.6 0.5 broadcast.45
  44.1 0.7 reduce.4
  44.8 0.1 eq.28
  44.9 0.2 fusion.9
  45.0 15.3 %all-to-all-done.1 = bf16[32,16,1024]{2,1,0:T(8,128)(2,1)S(1)} async-done(((bf16[32,16,1024]{2,1,0:T(8,128)(2,1)}), bf16[32,16,1024]{2,1,0:T(8,128)(2,1)S(1)}, u32[]{:S(2)}, u32[]{:S(2)}) %all-to-all-start.1) | async-done | bytes 1048608 | tf_op jit(solution)/shard_map/all_to_all | solution.py:63
  60.3 0.3 fusion.8
  60.6 0.0 copy-done.1
  60.6 0.0 copy-done.5
  60.7 3.0 multiply_reduce_fusion.1
  63.7 0.8 multiply_convert_fusion.4
  64.5 0.0 all-gather.2.cloned.1.call-update
  64.5 0.2 reduce-scatter.2.cloned.1.call-start
  64.8 0.0 copy-done.4
  64.8 0.0 copy-done.6
  64.8 0.1 copy.28
  64.9 0.1 reshape.70
  65.0 0.0 copy-done.2
  65.0 0.1 copy.29
  65.1 0.1 reshape.71
  65.3 0.0 copy-done.3
  65.3 0.1 copy.31
  65.4 0.1 mul.63
  65.5 51.0 %all-gather.2.cloned.1.call-done = bf16[4096,1024]{1,0:T(8,128)(2,1)} async-done(((bf16[128,1024]{1,0:T(8,128)(2,1)}), bf16[4096,1024]{1,0:T(8,128)(2,1)}) %all-gather.2.cloned.1.call-update) | async-done | bytes 8388624 | tf_op jit(solution)/shard_map/all_gather | solution.py:100
  116.5 11.9 %fusion.3 = bf16[1088,1024]{1,0:T(8,128)(2,1)S(1)} fusion(bf16[4096,1024]{1,0:T(8,128)(2,1)} %all-gather.2.cloned.1.call-done, s32[1088]{0:T(1024)S(1)} %pad_add_fusion), kind=kOutput, calls=%fused_computation.15 | convolution fusion | flops 9132376064 | bytes 10621184 | tf_op jit(solution)/shard_map/dot_general | solution.py:104
  128.4 1.4 slice.21
  129.8 0.1 reshape.72
  129.9 3.7 reshape.73
  133.6 0.4 fusion.27
  134.0 0.1 fusion.26
  134.1 2.6 pad_maximum_fusion.3
  136.6 0.0 copy-start.7
  136.7 0.7 fusion.2
  137.4 0.3 broadcast_in_dim.44
  137.7 12.6 %convert_reduce_fusion = (f32[1024]{0:T(1024)S(1)}, bf16[1024,1024]{1,0:T(8,128)(2,1)S(1)}, f32[1024]{0:T(1024)S(1)}, bf16[1024,1024]{1,0:T(8,128)(2,1)}) fusion(f32[1024]{0:T(1024)S(1)} %copy-done.7, f32[1024]{0:T(1024)S(1)} %convert_element_type.53, f32[1024]{0:T(1024)S(1)} %mul.63, bf16[3072,1024]{1,0:T(8,128)(2,1)} %param.26, ...), kind=kOutput, calls=%fused_computation.11 | convolution fusion | flops 6480197632 | bytes 16797696 | tf_op jit(solution)/shard_map/dot_general | solution.py:15
  150.2 11.3 %fusion.4 = f32[3072,1024]{1,0:T(8,128)} fusion(bf16[1024,1024]{1,0:T(8,128)(2,1)S(1)} %get-tuple-element.20, bf16[1024,1024]{1,0:T(8,128)(2,1)S(1)} %fusion.2, bf16[1024,1024]{1,0:T(8,128)(2,1)S(1)} %bitcast.32, bf16[1024,1024]{1,0:T(8,128)(2,1)S(1)} %bitcast.34), kind=kOutput, calls=%fused_computation.16 | convolution fusion | flops 6461325312 | bytes 20971520 | tf_op jit(solution)/shard_map/dot_general | solution.py:26
  161.6 0.0 reduce-scatter.2.cloned.1.call-update
  161.6 64.8 %all-reduce.2 = (f32[1024]{0:T(1024)S(1)}, f32[1024]{0:T(1024)S(1)}) all-reduce(f32[1024]{0:T(1024)S(1)} %get-tuple-element.19, f32[1024]{0:T(1024)S(1)} %get-tuple-element.23), channel_id=3, replica_groups=mesh['pair'=4,'node'=32] {'pair','node'}, use_global_device_ids=true, to_apply=%region_6.7.clone | all-reduce | flops 2048 | bytes 16384
  226.5 0.6 dynamic-slice
  227.0 0.6 dynamic-slice.1
  227.6 2.3 fusion.28
  229.9 0.1 reshape.74
  230.0 0.7 copy.32
  230.7 150.2 %reduce-scatter.2.cloned.1.call-done = f32[24,1024]{1,0:T(8,128)} async-done(((f32[3072,1024]{1,0:T(8,128)}), f32[24,1024]{1,0:T(8,128)}) %reduce-scatter.2.cloned.1.call-update) | async-done | bytes 98320 | tf_op jit(solution)/shard_map/reduce_scatter | solution.py:110
  (11 shorter events, 0.1 us)
Async XLA Ops:
  7.2 12.4 %copy-start = (bf16[1024,1024]{1,0:T(8,128)(2,1)S(1)}, bf16[1024,1024]{1,0:T(8,128)(2,1)}, u32[]{:S(2)}) copy-start(bf16[1024,1024]{1,0:T(8,128)(2,1)} %param.16) | copy-start | bytes 6291460
  11.0 15.5 %all-to-all-start.2 = ((bf16[32,1,16]{2,1,0:T(2,128)(2,1)}), bf16[32,1,16]{2,1,0:T(2,128)(2,1)S(1)}, u32[]{:S(2)}, u32[]{:S(2)}) async-start(bf16[32,1,16]{2,1,0:T(2,128)(2,1)} %all_to_all.20), calls=%async_computation.2 | async-start | bytes 32768 | tf_op jit(solution)/shard_map/all_to_all | solution.py:70
  19.6 41.0 %copy-start.1 = (bf16[128,1024]{1,0:T(8,128)(2,1)S(1)}, bf16[128,1024]{1,0:T(8,128)(2,1)}, u32[]{:S(2)}) copy-start(bf16[128,1024]{1,0:T(8,128)(2,1)} %param.15) | copy-start | bytes 786436
  19.6 41.0 %copy-start.5 = (f32[1024]{0:T(1024)S(1)}, f32[1024]{0:T(1024)}, u32[]{:S(2)}) copy-start(f32[1024]{0:T(1024)} %param.23) | copy-start | bytes 12292
  26.5 11.8 %all-to-all-start = ((s32[32,1,16]{2,1,0:T(1,128)}), s32[32,1,16]{2,1,0:T(1,128)S(1)}, u32[]{:S(2)}, u32[]{:S(2)}) async-start(s32[32,1,16]{2,1,0:T(1,128)} %bitcast), calls=%async_computation | async-start | bytes 32768 | tf_op jit(solution)/shard_map/all_to_all | solution.py:77
  38.3 22.0 %all-to-all-start.1 = ((bf16[32,16,1024]{2,1,0:T(8,128)(2,1)}), bf16[32,16,1024]{2,1,0:T(8,128)(2,1)S(1)}, u32[]{:S(2)}, u32[]{:S(2)}) async-start(bf16[32,16,1024]{2,1,0:T(8,128)(2,1)} %bitcast.1), calls=%async_computation.1 | async-start | bytes 2097152 | tf_op jit(solution)/shard_map/all_to_all | solution.py:63
  43.4 73.1 %all-gather.2.cloned.1.call-start = ((), (), s32[]{:S(2)}) async-start(), calls=%async_computation.4 | async-start | bytes 8650752 | tf_op jit(solution)/shard_map/all_gather | solution.py:100
  60.3 4.5 %copy-start.4 = (bf16[1024]{0:T(1024)(128)(2,1)S(1)}, bf16[1024]{0:T(1024)(128)(2,1)}, u32[]{:S(2)}) copy-start(bf16[1024]{0:T(1024)(128)(2,1)} %param.28) | copy-start | bytes 6148
  60.3 4.5 %copy-start.6 = (s32[64,2]{0,1:T(2,128)S(1)}, s32[64,2]{0,1:T(2,128)}, u32[]{:S(2)}) copy-start(s32[64,2]{0,1:T(2,128)} %param.24) | copy-start | bytes 1540
  60.3 4.7 %copy-start.2 = (s32[64,15]{0,1:T(8,128)S(1)}, s32[64,15]{0,1:T(8,128)}, u32[]{:S(2)}) copy-start(s32[64,15]{0,1:T(8,128)} %param.25) | copy-start | bytes 11524
  60.3 5.0 %copy-start.3 = (f32[64,16]{0,1:T(8,128)S(1)}, f32[64,16]{0,1:T(8,128)}, u32[]{:S(2)}) copy-start(f32[64,16]{0,1:T(8,128)} %param.29) | copy-start | bytes 12292
  64.5 316.4 %reduce-scatter.2.cloned.1.call-start = ((), (), s32[]{:S(2)}) async-start(), calls=%async_computation.5 | async-start | bytes 12681216 | tf_op jit(solution)/shard_map/reduce_scatter | solution.py:110
  136.6 1.0 copy-start.7
Sparse Core Ops, SparseCore 0:
  64.7 51.7 all-gather.1
  161.7 219.1 reduce-scatter.1
where the time goes:
time: 390 us; the launch traced here: 388 us
  waiting for transfers between devices  221 us (57%)
  blocking collectives  64.8 us (17%)
  matrix products  43 us (11%)
  starting transfers between devices  18.9 us (5%)
  local copies, waits for them, and re-layouts  14.4 us (4%)
  between operations  14.3 us (4%)
  other arithmetic  11 us (3%)
    reduce_scatter x1, waiting for transfers between devices, body(): lax.psum_scatter(grad_weight, ('pair', 'node'), scatter_dimension=0, tile...  150 us
    unnamed x1, blocking collectives  64.8 us
    all_gather x1, waiting for transfers between devices, body(): shard_rows = lax.all_gather(embedding, 'node', axis=0, tiled=True)  51 us
    all_to_all x1, waiting for transfers between devices, body(): lax.all_to_all(buffer.reshape(node_count, slot_count, feature_dim), 'node...  15.3 us
    dot_general x1, matrix products, score_pairs(): jnp.dot(inputs, hidden_weight, preferred_element_type=jnp.float32)  12.6 us
    dot_general x1, matrix products, body(): gathered = jnp.dot(onehot, shard_rows, preferred_element_type=jnp.float32)  11.9 us
    dot_general x1, matrix products, score_pairs(): lax.dot_general(inputs, pre_grad, (((0,), (0,)), ((), ())), preferred_ele...  11.3 us
    all_to_all x1, starting transfers between devices, body(): lax.all_to_all(weight_slots.reshape(node_count, slot_count), 'node', spli...  8.59 us
  transfers between devices with their start and end apart: 5, of which 5 were waited for; matrix products, arithmetic and copies ran while one was open for 4% of the time, Pallas kernels for 0%

commit v1 on v0

--- a/solution.py
+++ b/solution.py
@@ -1,32 +1,353 @@
+import functools
 import jax
 import jax.numpy as jnp
 from jax import lax
+from jax.experimental import pallas as pl
+from jax.experimental.pallas import tpu as pltpu
 from jax.sharding import PartitionSpec as P
 
-
-def score_pairs(fetched, pairs_dev, hidden_weight, hidden_bias, score_weight, score_cot):
-    feature_dim = fetched.shape[1]
-    query = fetched[: 2 * pairs_dev].reshape(pairs_dev, 2, feature_dim)
-    negatives = fetched[2 * pairs_dev :].reshape(pairs_dev, -1, feature_dim)
-    cand_rows = jnp.concatenate([query[:, 1:2, :], negatives], axis=1)
-    query_full = jnp.broadcast_to(query[:, 0:1, :], cand_rows.shape)
-    product = (query_full.astype(jnp.float32) * cand_rows.astype(jnp.float32)).astype(jnp.bfloat16)
-    inputs = jnp.concatenate([query_full, cand_rows, product], axis=-1).reshape(-1, 3 * feature_dim)
-    pre_act = jnp.dot(inputs, hidden_weight, preferred_element_type=jnp.float32) + hidden_bias
-    sigmoid_pre = jax.nn.sigmoid(pre_act)
-    hidden = (pre_act * sigmoid_pre).astype(jnp.bfloat16)
-    scores = jnp.dot(hidden, score_weight, preferred_element_type=jnp.float32)
-    cot_flat = score_cot.reshape(-1)
-    grad_score = jnp.sum(cot_flat[:, None] * hidden.astype(jnp.float32), axis=0)
-    hidden_grad = cot_flat[:, None] * score_weight.astype(jnp.float32)[None, :]
-    pre_grad = (hidden_grad * sigmoid_pre * (1.0 + pre_act * (1.0 - sigmoid_pre))).astype(
-        jnp.bfloat16
-    )
-    grad_bias = jnp.sum(pre_grad.astype(jnp.float32), axis=0)
-    grad_weight = lax.dot_general(
-        inputs, pre_grad, (((0,), (0,)), ((), ())), preferred_element_type=jnp.float32
-    )
-    return (scores.reshape(pairs_dev, -1), grad_weight, grad_bias, grad_score)
+MESH = pl.DeviceIdType.MESH
+F32 = jnp.float32
+BF16 = jnp.bfloat16
+ORDERS = (("z", "x", "y"), ("x", "y", "z"), ("y", "z", "x"))
+
+
+def place():
+    node = lax.axis_index("node")
+    return {
+        "z": lax.axis_index("pair"),
+        "x": node // 8,
+        "y": (node // 2) % 4,
+        "c": node % 2,
+    }
+
+
+def device(at, **other):
+    pos = dict(at, **other)
+    return (pos["z"], pos["x"] * 8 + pos["y"] * 2 + pos["c"])
+
+
+def ring(at, axis, step):
+    return device(at, **{axis: (at[axis] + step) % 4})
+
+
+def part(ref, third, **sel):
+    full = pl.ds(0, 4)
+    return ref.at[sel.get("z", full), sel.get("x", full), sel.get("y", full), third]
+
+
+def spot(n):
+    chip = n // 3
+    return (chip // 16, (chip // 4) % 4, chip % 4, n % 3)
+
+
+class Links:
+    def __init__(self, send_sem, recv_sem):
+        self.send_sem, self.recv_sem, self.count, self.copies = send_sem, recv_sem, 0, []
+
+    def start(self, src, dst, to):
+        copy = pltpu.make_async_remote_copy(
+            src_ref=src,
+            dst_ref=dst,
+            send_sem=self.send_sem.at[self.count],
+            recv_sem=self.recv_sem.at[self.count],
+            device_id=to,
+            device_id_type=MESH,
+        )
+        copy.start()
+        self.count += 1
+        self.copies.append(copy)
+        return copy
+
+    def drop(self, done):
+        self.copies = [copy for copy in self.copies if copy is not done]
+
+    def drain(self):
+        for copy in self.copies:
+            copy.wait_send()
+
+
+def meet(partners):
+    barrier = pltpu.get_barrier_semaphore()
+    for to in partners:
+        pl.semaphore_signal(barrier, inc=1, device_id=to, device_id_type=MESH)
+    pl.semaphore_wait(barrier, len(partners))
+
+
+def add_into(dst, *srcs):
+    total = dst[...].astype(F32)
+    for src in srcs:
+        total = total + src[...].astype(F32)
+    dst[...] = total.astype(dst.dtype)
+
+
+def score_kernel(
+    q_ref, cand_ref, hw_ref, hb_ref, sw_ref, sg_ref,
+    scores_ref, gw_ref, aux_out_ref,
+    q2, gq2, prod, grad, query_act, acc_bias, acc_score,
+    own, give, take,
+    opp1, near1, opp2, near2, last3, final, final_in,
+    aux, aux_core, aux_in,
+    core_send, core_recv, send_sem, recv_sem,
+):
+    at = place()
+    core = at["c"]
+    partners = [device(at, c=1 - core)]
+    for axis in ("x", "y", "z"):
+        for step in (1, 2, 3):
+            partners.append(ring(at, axis, step))
+    meet(partners)
+    sibling = partners[0]
+    links = Links(send_sem, recv_sem)
+
+    query = q_ref[...]
+    q2[pl.ds(0, 64)] = query
+    q2[pl.ds(64, 64)] = query
+    query_act[...] = jnp.dot(query, hw_ref[pl.ds(0, 1024)], preferred_element_type=F32) + hb_ref[...]
+    acc_bias[...] = jnp.zeros_like(acc_bias)
+    acc_score[...] = jnp.zeros_like(acc_score)
+    scores_ref[...] = jnp.zeros_like(scores_ref)
+
+    def forward(i, query_grad):
+        rows = pl.ds(pl.multiple_of(i * 256, 256), 256)
+        cand = cand_ref[rows]
+        query = q_ref[...]
+        product = (cand.astype(F32).reshape(4, 64, 1024) * query.astype(F32)[None]).astype(BF16).reshape(256, 1024)
+        prod[rows] = product
+        act = jnp.dot(cand, hw_ref[pl.ds(1024, 1024)], preferred_element_type=F32)
+        act = act + jnp.dot(product, hw_ref[pl.ds(2048, 1024)], preferred_element_type=F32)
+        sw = sw_ref[...].astype(F32)
+        sg = sg_ref[...]
+        lane = lax.broadcasted_iota(jnp.int32, (64, 16), 1)
+        score = scores_ref[...]
+        bias_sum = acc_bias[...]
+        score_sum = acc_score[...]
+        for k in range(4):
+            mine = lane == i * 4 + k
+            x = act[k * 64 : (k + 1) * 64] + query_act[...]
+            s = 0.5 * jnp.tanh(0.5 * x) + 0.5
+            hidden = (x * s).astype(BF16).astype(F32)
+            score = score + jnp.where(mine, jnp.sum(hidden * sw, axis=1, keepdims=True), 0.0)
+            cot = jnp.sum(jnp.where(mine, sg, 0.0), axis=1, keepdims=True)
+            score_sum = score_sum + jnp.sum((cot * hidden).reshape(8, 8, 1024), axis=0)
+            pre_grad = (cot * sw * s * (1.0 + x * (1.0 - s))).astype(BF16)
+            grad[pl.ds(pl.multiple_of(i * 256 + k * 64, 64), 64)] = pre_grad
+            pre_grad = pre_grad.astype(F32)
+            bias_sum = bias_sum + jnp.sum(pre_grad.reshape(8, 8, 1024), axis=0)
+            query_grad = query_grad + pre_grad
+        scores_ref[...] = score
+        acc_bias[...] = bias_sum
+        acc_score[...] = score_sum
+        return query_grad
+
+    query_grad = lax.fori_loop(0, 4, forward, jnp.zeros((64, 1024), F32))
+    high = query_grad.astype(BF16)
+    gq2[pl.ds(0, 64)] = high
+    gq2[pl.ds(64, 64)] = (query_grad - high.astype(F32)).astype(BF16)
+    aux[pl.ds(0, 1)] = jnp.sum(acc_bias[...], axis=0, keepdims=True)
+    aux[pl.ds(1, 1)] = jnp.sum(acc_score[...], axis=0, keepdims=True)
+    aux_core_copy = links.start(aux, aux_core, sibling)
+
+    def core_copy(j):
+        blocks = pl.ds(j * 16, 16)
+        return pltpu.make_async_remote_copy(
+            src_ref=give.at[blocks],
+            dst_ref=take.at[blocks],
+            send_sem=core_send.at[j],
+            recv_sem=core_recv.at[j],
+            device_id=sibling,
+            device_id_type=MESH,
+        )
+
+    my_cols = pl.ds(pl.multiple_of(core * 512, 512), 512)
+    other_cols = pl.ds(pl.multiple_of((1 - core) * 512, 512), 512)
+    contract = (((0,), (0,)), ((), ()))
+
+    def chunk(j, x_ref, g_ref, k):
+        x = x_ref[:, pl.ds(pl.multiple_of(k * 256, 256), 256)]
+        other = lax.dot_general(x, g_ref[:, other_cols], contract, preferred_element_type=F32)
+        give[pl.ds(j * 16, 16)] = other.astype(BF16).reshape(16, 16, 512)
+        core_copy(j).start()
+        mine = lax.dot_general(x, g_ref[:, my_cols], contract, preferred_element_type=F32)
+        mine = mine.astype(BF16)
+        for b in range(16):
+            own[spot(j * 16 + b)] = mine[b * 16 : (b + 1) * 16]
+
+    def land(j):
+        core_copy(j).wait_recv()
+        for b in range(16):
+            n = j * 16 + b
+            own[spot(n)] = (own[spot(n)].astype(F32) + take[n].astype(F32)).astype(BF16)
+
+    def weight_c(k, carry):
+        chunk(k + 4, cand_ref, grad, k)
+        return carry
+
+    def weight_p(k, carry):
+        chunk(k + 8, prod, grad, k)
+        land(k + 4)
+        return carry
+
+    def weight_q(k, carry):
+        chunk(k, q2, gq2, k)
+        land(k + 8)
+        return carry
+
+    def weight_last(k, carry):
+        land(k)
+        return carry
+
+    lax.fori_loop(0, 4, weight_c, 0)
+    lax.fori_loop(0, 4, weight_p, 0)
+    lax.fori_loop(0, 4, weight_q, 0)
+    aux_core_copy.wait()
+    links.drop(aux_core_copy)
+    add_into(aux, aux_core)
+    lax.fori_loop(0, 4, weight_last, 0)
+
+    low, high_half = pl.ds(0, 2), pl.ds(2, 2)
+
+    def aux_start(stage):
+        axis = ("x", "y", "z")[stage]
+        return [
+            links.start(aux, aux_in.at[stage * 3 + d - 1], ring(at, axis, d)) for d in (1, 2, 3)
+        ]
+
+    def aux_add(stage, copies):
+        for copy in copies:
+            copy.wait()
+            links.drop(copy)
+        add_into(aux, *[aux_in.at[stage * 3 + d - 1] for d in (1, 2, 3)])
+
+    def first_sends(view, opp, near, axis):
+        me = at[axis]
+        right, left = ring(at, axis, 1), ring(at, axis, 3)
+        far = (me + 2) % 4
+        a = links.start(view(far, high_half), opp.at[0], right)
+        b = links.start(view(far, low), opp.at[1], left)
+        c = links.start(view((me + 1) % 4, low), near.at[0, low], right)
+        d = links.start(view((me + 3) % 4, high_half), near.at[1, high_half], left)
+        return [a, b, c, d]
+
+    def second_sends(view, opp, near, axis, copies):
+        me = at[axis]
+        right, left = ring(at, axis, 1), ring(at, axis, 3)
+        copies[0].wait_recv()
+        add_into(view((me + 1) % 4, high_half), opp.at[0])
+        copies.append(links.start(view((me + 1) % 4, high_half), near.at[0, high_half], right))
+        copies[1].wait_recv()
+        add_into(view((me + 3) % 4, low), opp.at[1])
+        copies.append(links.start(view((me + 3) % 4, low), near.at[1, low], left))
+
+    def finish(view, near, axis, copies):
+        for copy in copies[2:]:
+            copy.wait_recv()
+        add_into(view(at[axis], pl.ds(0, 4)), near.at[0], near.at[1])
+
+    def view1(third):
+        axis = ORDERS[third][0]
+        halved = "x" if axis == "z" else "z"
+        return lambda i, h: part(own, third, **{axis: i, halved: h})
+
+    def view2(third):
+        a, b, c = ORDERS[third]
+        return lambda i, h: part(own, third, **{a: at[a], b: i, c: h})
+
+    small = aux_start(0)
+    one = [first_sends(view1(t), opp1.at[t], near1.at[t], ORDERS[t][0]) for t in range(3)]
+    for t in range(3):
+        second_sends(view1(t), opp1.at[t], near1.at[t], ORDERS[t][0], one[t])
+    aux_add(0, small)
+    small = aux_start(1)
+    two = []
+    for t in range(3):
+        finish(view1(t), near1.at[t], ORDERS[t][0], one[t])
+        two.append(first_sends(view2(t), opp2.at[t], near2.at[t], ORDERS[t][1]))
+    for t in range(3):
+        second_sends(view2(t), opp2.at[t], near2.at[t], ORDERS[t][1], two[t])
+    aux_add(1, small)
+    small = aux_start(2)
+    three = []
+    for t in range(3):
+        finish(view2(t), near2.at[t], ORDERS[t][1], two[t])
+        a, b, c = ORDERS[t]
+        three.append(
+            [
+                links.start(
+                    part(own, t, **{a: at[a], b: at[b], c: (at[c] + d) % 4}),
+                    last3.at[t, d - 1],
+                    ring(at, c, d),
+                )
+                for d in (1, 2, 3)
+            ]
+        )
+    for t in range(3):
+        total = part(own, t, z=at["z"], x=at["x"], y=at["y"])[...].astype(F32)
+        for d in (1, 2, 3):
+            three[t][d - 1].wait_recv()
+            total = total + last3[t, d - 1].astype(F32)
+        final[pl.ds(t * 16, 16)] = total
+    swap = links.start(final.at[pl.ds(pl.multiple_of((1 - core) * 24, 8), 24)], final_in, sibling)
+    gw_ref[:, my_cols] = final[pl.ds(pl.multiple_of(core * 24, 8), 24)]
+
+    aux_add(2, small)
+    aux_out_ref[...] = aux[...]
+    swap.wait_recv()
+    gw_ref[:, other_cols] = final_in[...]
+    lax.fori_loop(0, 12, lambda j, carry: (core_copy(j).wait_send(), carry)[1], 0)
+    links.drain()
+
+
+def score_reduce(query, cand, hidden_weight, hidden_bias, score_weight, score_grad):
+    vmem = pl.BlockSpec(memory_space=pltpu.VMEM)
+    return pl.pallas_call(
+        score_kernel,
+        out_shape=(
+            jax.ShapeDtypeStruct((64, 16), F32),
+            jax.ShapeDtypeStruct((24, 1024), F32),
+            jax.ShapeDtypeStruct((2, 1024), F32),
+        ),
+        in_specs=[vmem] * 6,
+        out_specs=(vmem, vmem, vmem),
+        scratch_shapes=[
+            pltpu.VMEM((128, 1024), BF16),
+            pltpu.VMEM((128, 1024), BF16),
+            pltpu.VMEM((1024, 1024), BF16),
+            pltpu.VMEM((1024, 1024), BF16),
+            pltpu.VMEM((64, 1024), F32),
+            pltpu.VMEM((8, 1024), F32),
+            pltpu.VMEM((8, 1024), F32),
+            pltpu.VMEM((4, 4, 4, 3, 16, 512), BF16),
+            pltpu.VMEM((192, 16, 512), BF16),
+            pltpu.VMEM((192, 16, 512), BF16),
+            pltpu.VMEM((3, 2, 2, 4, 16, 512), BF16),
+            pltpu.VMEM((3, 2, 4, 4, 16, 512), BF16),
+            pltpu.VMEM((3, 2, 2, 16, 512), BF16),
+            pltpu.VMEM((3, 2, 4, 16, 512), BF16),
+            pltpu.VMEM((3, 3, 16, 512), BF16),
+            pltpu.VMEM((48, 512), F32),
+            pltpu.VMEM((24, 512), F32),
+            pltpu.VMEM((2, 1024), F32),
+            pltpu.VMEM((2, 1024), F32),
+            pltpu.VMEM((9, 2, 1024), F32),
+            pltpu.SemaphoreType.DMA((12,)),
+            pltpu.SemaphoreType.DMA((12,)),
+            pltpu.SemaphoreType.DMA((64,)),
+            pltpu.SemaphoreType.DMA((64,)),
+        ],
+        compiler_params=pltpu.CompilerParams(
+            collective_id=0, has_side_effects=True, vmem_limit_bytes=48 * 2**20
+        ),
+        cost_estimate=pl.CostEstimate(flops=13 * 10**9, bytes_accessed=12 * 10**6, transcendentals=10**6),
+        name="score_reduce",
+    )(
+        query,
+        cand,
+        hidden_weight,
+        hidden_bias.reshape(1, 1024),
+        score_weight.astype(F32).reshape(1, 1024),
+        score_grad,
+    )
 
 
 def body(
@@ -95,22 +416,19 @@
     embedding = (
         rectified * lax.rsqrt(jnp.mean(rectified * rectified, axis=-1, keepdims=True) + 1e-06)
     ).astype(jnp.bfloat16)
-    pairs_dev = pair_ids.shape[0]
-    ask_ids = jnp.concatenate([pair_ids.reshape(-1), neg_ids.reshape(-1)])
+    cand_ids = jnp.concatenate([pair_ids[:, 1:2], neg_ids], axis=1).T.reshape(-1)
+    ask_ids = jnp.concatenate([pair_ids[:, 0], cand_ids])
     shard_rows = lax.all_gather(embedding, "node", axis=0, tiled=True)
     onehot = (ask_ids[:, None] == jnp.arange(shard_rows.shape[0], dtype=jnp.int32)[None, :]).astype(
         jnp.bfloat16
     )
-    gathered = jnp.dot(onehot, shard_rows, preferred_element_type=jnp.float32)
-    fetched = gathered.astype(jnp.bfloat16)
-    scores, grad_weight, grad_bias, grad_score = score_pairs(
-        fetched, pairs_dev, hidden_weight, hidden_bias, score_weight, score_grad
-    )
-    shared_weight, shared_bias, shared_score = (
-        lax.psum_scatter(grad_weight, ("pair", "node"), scatter_dimension=0, tiled=True),
-        lax.psum_scatter(grad_bias, ("pair", "node"), scatter_dimension=0, tiled=True),
-        lax.psum_scatter(grad_score, ("pair", "node"), scatter_dimension=0, tiled=True),
-    )
+    fetched = jnp.dot(onehot, shard_rows, preferred_element_type=jnp.float32).astype(jnp.bfloat16)
+    scores, shared_weight, aux = score_reduce(
+        fetched[:64], fetched[64:], hidden_weight, hidden_bias, score_weight, score_grad
+    )
+    index = lax.axis_index("pair") * 32 + lax.axis_index("node")
+    mine = lax.dynamic_slice(aux, (0, index * 8), (2, 8))
+    shared_bias, shared_score = mine[0], mine[1]
     return (embedding, scores, shared_weight, shared_bias, shared_score)
 
 

time: 390 us -> 192 us (0.49)
  waiting for transfers between devices: 221 us -> 71.6 us
  blocking collectives: 64.8 us -> 0 us
  Pallas kernels: 0 us -> 53.6 us
  matrix products: 43 us -> 16.8 us
  local copies, waits for them, and re-layouts: 14.4 us -> 8.67 us
    reduce_scatter x1 -> x0, waiting for transfers between devices: 150 us -> none  [body(): lax.psum_scatter(grad_weight, ('pair', 'node'), scatter_dimension=0, tile...]
    unnamed x1 -> x0, blocking collectives: 64.8 us -> none
    pallas_call x0 -> x1, Pallas kernels: none -> 53.6 us  [score_reduce(): pl.pallas_call(score_kernel, out_shape=(jax.ShapeDtypeStruct((64, 16), F3...]
    dot_general x4 -> x1, matrix products: 38.1 us -> 11.9 us  [body(): jnp.dot(onehot, shard_rows, preferred_element_type=jnp.float32)]
    reshape x5 -> x1, local copies, waits for them, and re-layouts: 4.18 us -> 0.07 us  [body(): jnp.concatenate([pair_ids[:, 1:2], neg_ids], axis=1).T.reshape(-1)]
  transfers between devices with their start and end apart: 5 -> 4, of which waited for: 5 -> 4; matrix products, arithmetic and copies ran while one was open for 4% -> 5% of each run, Pallas kernels for 0% -> 0%
where the time goes in v1:
time: 192 us; the launch traced here: 191 us
  waiting for transfers between devices  71.6 us (37%)
  Pallas kernels  53.6 us (28%)
  starting transfers between devices  18.7 us (10%)
  matrix products  16.8 us (9%)
  between operations  14.3 us (7%)
  local copies, waits for them, and re-layouts  8.67 us (5%)
  other arithmetic  7.72 us (4%)
    pallas_call x1, Pallas kernels, score_reduce(): pl.pallas_call(score_kernel, out_shape=(jax.ShapeDtypeStruct((64, 16), F3...  53.6 us
    all_gather x1, waiting for transfers between devices, body(): shard_rows = lax.all_gather(embedding, 'node', axis=0, tiled=True)  51.6 us
    all_to_all x1, waiting for transfers between devices, body(): lax.all_to_all(buffer.reshape(node_count, slot_count, feature_dim), 'node...  15.3 us
    dot_general x1, matrix products, body(): jnp.dot(onehot, shard_rows, preferred_element_type=jnp.float32)  11.9 us
    all_to_all x1, starting transfers between devices, body(): lax.all_to_all(weight_slots.reshape(node_count, slot_count), 'node', spli...  8.59 us
    all_to_all x1, starting transfers between devices, body(): lax.all_to_all(buffer.reshape(node_count, slot_count, feature_dim), 'node...  5.09 us
    all_to_all x1, starting transfers between devices, body(): lax.all_to_all(target_slots.reshape(node_count, slot_count), 'node', spli...  4.94 us
    scatter x1, other arithmetic, body(): jnp.zeros((slot_total, feature_dim), jnp.bfloat16).at[edge_slot]  3.89 us
  transfers between devices with their start and end apart: 4, of which 4 were waited for; matrix products, arithmetic and copies ran while one was open for 5% of the time, Pallas kernels for 0%

profile of v1, /device:TPU:1, one launch (start us, length us, event | category | flops | bytes accessed | tf_op | source)
XLA Modules:
  0.0 191.4 jit_solution(9119827413633097916)
XLA Ops:
  7.2 0.0 copy-start
  7.2 0.8 compare_select_fusion.1
  8.0 2.3 %scatter_custom_fusion.2 = bf16[512]{0:T(512)(128)(2,1)S(1)} fusion(s32[256]{0:T(256)S(1)} %compare_select_fusion.1, bf16[256]{0:T(256)(128)(2,1)} %param.21, bf16[]{:T(256)} %constant.16.clone.1), kind=kCustom, calls=%fused_computation.39 | custom fusion | bytes 1536 | tf_op jit(solution)/shard_map/scatter | solution.py:381
  10.3 0.7 all_to_all.20
  11.0 8.6 %all-to-all-start.2 = ((bf16[32,1,16]{2,1,0:T(2,128)(2,1)}), bf16[32,1,16]{2,1,0:T(2,128)(2,1)S(1)}, u32[]{:S(2)}, u32[]{:S(2)}) async-start(bf16[32,1,16]{2,1,0:T(2,128)(2,1)} %all_to_all.20), calls=%async_computation.2 | async-start | bytes 32768 | tf_op jit(solution)/shard_map/all_to_all | solution.py:391
  19.6 0.0 copy-done
  19.6 0.0 copy-start.2
  19.6 0.0 copy-start.5
  19.6 1.4 fusion.4
  21.1 0.7 compare_select_fusion
  21.8 1.6 scatter_custom_fusion
  23.3 0.7 all_to_all.15
  24.0 2.4 %all-to-all-done.2 = bf16[32,1,16]{2,1,0:T(2,128)(2,1)S(1)} async-done(((bf16[32,1,16]{2,1,0:T(2,128)(2,1)}), bf16[32,1,16]{2,1,0:T(2,128)(2,1)S(1)}, u32[]{:S(2)}, u32[]{:S(2)}) %all-to-all-start.2) | async-done | bytes 1056 | tf_op jit(solution)/shard_map/all_to_all | solution.py:391
  26.5 4.9 %all-to-all-start = ((s32[32,1,16]{2,1,0:T(1,128)}), s32[32,1,16]{2,1,0:T(1,128)S(1)}, u32[]{:S(2)}, u32[]{:S(2)}) async-start(s32[32,1,16]{2,1,0:T(1,128)} %bitcast), calls=%async_computation | async-start | bytes 32768 | tf_op jit(solution)/shard_map/all_to_all | solution.py:398
  31.4 0.7 convert_element_type.18
  32.1 3.9 %scatter_custom_fusion.1 = bf16[512,1024]{1,0:T(8,128)(2,1)} fusion(s32[256]{0:T(256)S(1)} %compare_select_fusion.1, f32[256]{0:T(256)S(1)} %convert_element_type.18, bf16[]{:T(256)} %constant.16.clone.1, f32[128,1024]{1,0:T(8,128)S(1)} %fusion.4, s32[1024]{0:T(1024)S(1)} %pad_clamp_fusion), kind=kCustom, calls=%fused_computation.17 | custom fusion | flops 524288 | bytes 1577986 | tf_op jit(solution)/shard_map/scatter | solution.py:380
  36.0 2.3 %all-to-all-done = s32[32,1,16]{2,1,0:T(1,128)S(1)} async-done(((s32[32,1,16]{2,1,0:T(1,128)}), s32[32,1,16]{2,1,0:T(1,128)S(1)}, u32[]{:S(2)}, u32[]{:S(2)}) %all-to-all-start) | async-done | bytes 2080 | tf_op jit(solution)/shard_map/all_to_all | solution.py:398
  38.3 5.1 %all-to-all-start.1 = ((bf16[32,16,1024]{2,1,0:T(8,128)(2,1)}), bf16[32,16,1024]{2,1,0:T(8,128)(2,1)S(1)}, u32[]{:S(2)}, u32[]{:S(2)}) async-start(bf16[32,16,1024]{2,1,0:T(8,128)(2,1)} %bitcast.1), calls=%async_computation.1 | async-start | bytes 2097152 | tf_op jit(solution)/shard_map/all_to_all | solution.py:384
  43.4 0.0 all-gather.2.cloned.1.call-start
  43.4 0.1 reduce.1
  43.5 0.1 reshape.99
  43.6 0.5 broadcast.35
  44.1 0.7 reduce.4
  44.8 0.1 eq.28
  44.9 0.2 fusion.6
  45.0 15.3 %all-to-all-done.1 = bf16[32,16,1024]{2,1,0:T(8,128)(2,1)S(1)} async-done(((bf16[32,16,1024]{2,1,0:T(8,128)(2,1)}), bf16[32,16,1024]{2,1,0:T(8,128)(2,1)S(1)}, u32[]{:S(2)}, u32[]{:S(2)}) %all-to-all-start.1) | async-done | bytes 1048608 | tf_op jit(solution)/shard_map/all_to_all | solution.py:384
  60.3 0.0 copy-start.7
  60.3 0.0 copy-start.4
  60.3 0.0 copy-start.3
  60.3 0.0 copy-start.6
  60.3 0.3 fusion.5
  60.6 0.0 copy-done.2
  60.6 0.0 copy-done.5
  60.6 3.0 %multiply_reduce_fusion = (f32[128]{0:T(128)S(1)}, f32[128,1024]{1,0:T(8,128)S(1)}) fusion(f32[1024]{0:T(1024)S(1)} %copy-done.5, bf16[2048,1024]{1,0:T(8,128)(2,1)} %param.22, bf16[128,1024]{1,0:T(8,128)(2,1)S(1)} %fusion.5, bf16[128,1024]{1,0:T(8,128)(2,1)S(1)} %copy-done.2), kind=kOutput, calls=%fused_computation.22 | convolution fusion | flops 538443648 | bytes 5247488 | tf_op jit(solution)/shard_map/dot_general | solution.py:414
  63.7 0.8 multiply_convert_fusion.2
  64.5 0.0 all-gather.2.cloned.1.call-update
  64.5 0.0 copy-done.7
  64.5 0.0 copy-done.4
  64.6 0.1 reshape.57
  64.6 0.0 copy-done.3
  64.6 0.1 copy.26.sg_ref
  64.7 0.0 copy-done.6
  64.7 0.1 pad_add_fusion
  64.8 51.6 %all-gather.2.cloned.1.call-done = bf16[4096,1024]{1,0:T(8,128)(2,1)} async-done(((bf16[128,1024]{1,0:T(8,128)(2,1)}), bf16[4096,1024]{1,0:T(8,128)(2,1)}) %all-gather.2.cloned.1.call-update) | async-done | bytes 8388624 | tf_op jit(solution)/shard_map/all_gather | solution.py:421
  116.4 11.9 %fusion.2 = bf16[1088,1024]{1,0:T(8,128)(2,1)S(1)} fusion(bf16[4096,1024]{1,0:T(8,128)(2,1)} %all-gather.2.cloned.1.call-done, s32[1088]{0:T(1024)S(1)} %pad_add_fusion), kind=kOutput, calls=%fused_computation.7 | convolution fusion | flops 9132376064 | bytes 10621184 | tf_op jit(solution)/shard_map/dot_general | solution.py:425
  128.3 0.0 copy-start.1
  128.3 0.2 slice.27.cand_ref
  128.5 0.5 copy-done.1
  129.0 53.6 %score_reduce.1 = (f32[64,16]{1,0:T(8,128)S(1)}, f32[24,1024]{1,0:T(8,128)S(1)}, f32[2,1024]{1,0:T(2,128)S(1)}) custom-call(bf16[64,1024]{1,0:T(8,128)(2,1)S(1)} %slice.26.q_ref, bf16[1024,1024]{1,0:T(8,128)(2,1)S(1)} %slice.27.cand_ref, bf16[3072,1024]{1,0:T(8,128)(2,1)} %hw_ref.1, f32[1,1024]{1,0:T(1,128)S(1)} %bitcast.24, f32[1,1024]{1,0:T(1,128)S(1)} %bitcast.23, ...), custom_call_target="tpu_custom_call" | custom-call | flops 12999999488 | bytes 12000000 | tf_op jit(solution)/shard_map/score_reduce/pallas_call | solution.py:303
  182.6 0.1 constant_dynamic-slice_fusion
  182.7 0.5 slice_bitcast_fusion
  183.2 0.7 copy.27
  183.9 0.6 copy.29
  (6 shorter events, 0.0 us)
Async XLA Ops:
  7.2 12.4 %copy-start = (bf16[1024,1024]{1,0:T(8,128)(2,1)S(1)}, bf16[1024,1024]{1,0:T(8,128)(2,1)}, u32[]{:S(2)}) copy-start(bf16[1024,1024]{1,0:T(8,128)(2,1)} %param.16) | copy-start | bytes 6291460
  11.0 15.5 %all-to-all-start.2 = ((bf16[32,1,16]{2,1,0:T(2,128)(2,1)}), bf16[32,1,16]{2,1,0:T(2,128)(2,1)S(1)}, u32[]{:S(2)}, u32[]{:S(2)}) async-start(bf16[32,1,16]{2,1,0:T(2,128)(2,1)} %all_to_all.20), calls=%async_computation.2 | async-start | bytes 32768 | tf_op jit(solution)/shard_map/all_to_all | solution.py:391
  19.6 41.0 %copy-start.2 = (bf16[128,1024]{1,0:T(8,128)(2,1)S(1)}, bf16[128,1024]{1,0:T(8,128)(2,1)}, u32[]{:S(2)}) copy-start(bf16[128,1024]{1,0:T(8,128)(2,1)} %param.15) | copy-start | bytes 786436
  19.6 41.0 %copy-start.5 = (f32[1024]{0:T(1024)S(1)}, f32[1024]{0:T(1024)}, u32[]{:S(2)}) copy-start(f32[1024]{0:T(1024)} %param.23) | copy-start | bytes 12292
  26.5 11.8 %all-to-all-start = ((s32[32,1,16]{2,1,0:T(1,128)}), s32[32,1,16]{2,1,0:T(1,128)S(1)}, u32[]{:S(2)}, u32[]{:S(2)}) async-start(s32[32,1,16]{2,1,0:T(1,128)} %bitcast), calls=%async_computation | async-start | bytes 32768 | tf_op jit(solution)/shard_map/all_to_all | solution.py:398
  38.3 22.0 %all-to-all-start.1 = ((bf16[32,16,1024]{2,1,0:T(8,128)(2,1)}), bf16[32,16,1024]{2,1,0:T(8,128)(2,1)S(1)}, u32[]{:S(2)}, u32[]{:S(2)}) async-start(bf16[32,16,1024]{2,1,0:T(8,128)(2,1)} %bitcast.1), calls=%async_computation.1 | async-start | bytes 2097152 | tf_op jit(solution)/shard_map/all_to_all | solution.py:384
  43.4 73.0 %all-gather.2.cloned.1.call-start = ((), (), s32[]{:S(2)}) async-start(), calls=%async_computation.3 | async-start | bytes 8650752 | tf_op jit(solution)/shard_map/all_gather | solution.py:421
  60.3 4.2 %copy-start.7 = (s32[64,2]{0,1:T(2,128)S(1)}, s32[64,2]{0,1:T(2,128)}, u32[]{:S(2)}) copy-start(s32[64,2]{0,1:T(2,128)} %param.24) | copy-start | bytes 1540
  60.3 4.2 %copy-start.4 = (s32[64,15]{0,1:T(8,128)S(1)}, s32[64,15]{0,1:T(8,128)}, u32[]{:S(2)}) copy-start(s32[64,15]{0,1:T(8,128)} %param.25) | copy-start | bytes 11524
  60.3 4.3 %copy-start.3 = (f32[64,16]{0,1:T(8,128)S(1)}, f32[64,16]{0,1:T(8,128)}, u32[]{:S(2)}) copy-start(f32[64,16]{0,1:T(8,128)} %param.29) | copy-start | bytes 12292
  60.3 4.4 %copy-start.6 = (bf16[1024]{0:T(1024)(128)(2,1)S(1)}, bf16[1024]{0:T(1024)(128)(2,1)}, u32[]{:S(2)}) copy-start(bf16[1024]{0:T(1024)(128)(2,1)} %param.28) | copy-start | bytes 6148
  128.3 0.7 copy-start.1
Sparse Core Ops, SparseCore 0:
  64.6 51.7 all-gather.1

commit v2 on v1

--- a/solution.py
+++ b/solution.py
@@ -67,13 +67,6 @@
             copy.wait_send()
 
 
-def meet(partners):
-    barrier = pltpu.get_barrier_semaphore()
-    for to in partners:
-        pl.semaphore_signal(barrier, inc=1, device_id=to, device_id_type=MESH)
-    pl.semaphore_wait(barrier, len(partners))
-
-
 def add_into(dst, *srcs):
     total = dst[...].astype(F32)
     for src in srcs:
@@ -81,24 +74,239 @@
     dst[...] = total.astype(dst.dtype)
 
 
-def score_kernel(
-    q_ref, cand_ref, hw_ref, hb_ref, sw_ref, sg_ref,
-    scores_ref, gw_ref, aux_out_ref,
+GATHER_UNITS = ((0, 5), (5, 5), (10, 6))
+
+
+def table(ref, half, units, **sel):
+    full = pl.ds(0, 4)
+    return ref.at[sel.get("z", full), sel.get("x", full), sel.get("y", full), half, pl.ds(*units)]
+
+
+def network_kernel(
+    feats_ref, mw_hbm, mb_ref, source_ref, slot_ref, target_ref, weight_ref,
+    uw_hbm, ub_ref, pair_ref, neg_ref, hw_hbm, hb_ref, sw_ref, sg_ref,
+    emb_ref, scores_ref, gw_ref, aux_out_ref,
+    mw, uw, hw_ref, outbox, inbox, avg_out, avg_in, rows_f, shared, keys, onehot, acc, q_ref, cand_ref,
     q2, gq2, prod, grad, query_act, acc_bias, acc_score,
     own, give, take,
     opp1, near1, opp2, near2, last3, final, final_in,
     aux, aux_core, aux_in,
-    core_send, core_recv, send_sem, recv_sem,
+    load_sem, msg_send, msg_recv, core_send, core_recv, send_sem, recv_sem,
 ):
     at = place()
     core = at["c"]
-    partners = [device(at, c=1 - core)]
-    for axis in ("x", "y", "z"):
-        for step in (1, 2, 3):
-            partners.append(ring(at, axis, step))
-    meet(partners)
-    sibling = partners[0]
+    node = lax.axis_index("node")
+    sibling = device(at, c=1 - core)
+    barrier = pltpu.get_barrier_semaphore()
+
+    def greet(k, carry):
+        pl.semaphore_signal(
+            barrier, inc=1, device_id=(at["z"], (node + k) % 32), device_id_type=MESH
+        )
+        return carry
+
+    lax.fori_loop(1, 32, greet, 0)
+    for step in (1, 2, 3):
+        pl.semaphore_signal(barrier, inc=1, device_id=ring(at, "z", step), device_id_type=MESH)
     links = Links(send_sem, recv_sem)
+
+    quarter = pl.ds(pl.multiple_of(at["z"] * 256, 256), 256)
+    load_mw = pltpu.make_async_copy(mw_hbm.at[:, quarter], mw, load_sem.at[0])
+    load_uw = pltpu.make_async_copy(uw_hbm, uw, load_sem.at[1])
+    load_hw = pltpu.make_async_copy(hw_hbm, hw_ref, load_sem.at[2])
+    load_mw.start()
+    load_uw.start()
+    load_hw.start()
+
+    def pick(cond):
+        return jnp.where(cond, 1.0, 0.0).astype(BF16)
+
+    row = lax.broadcasted_iota(jnp.int32, (128, 256), 0)
+    weight = weight_ref[...]
+    target = target_ref[...].astype(F32)
+    from_node = jnp.where(row == source_ref[...], weight, 0.0)
+    beside = jnp.where(row == 0, weight, jnp.where(row == 1, target, 0.0))
+    edge_rows = jnp.concatenate([from_node, beside], axis=0).astype(BF16)
+    to_slot = pick(lax.broadcasted_iota(jnp.int32, (512, 256), 0) == slot_ref[...])
+    routed = lax.dot_general(
+        to_slot, edge_rows, (((1,), (1,)), ((), ())), preferred_element_type=F32
+    ).astype(BF16)
+    load_mw.wait()
+    project = jnp.dot(feats_ref[...], mw[...], preferred_element_type=F32) + mb_ref[:, quarter]
+    project = jnp.maximum(project, 0.0).astype(BF16)
+    message = jnp.dot(routed[:, :128], project, preferred_element_type=F32).astype(BF16)
+    outbox[:, :, pl.ds(0, 256)] = message.reshape(32, 16, 256)
+    outbox[:, :, pl.ds(256, 128)] = routed[:, 128:].reshape(32, 16, 128)
+    pl.semaphore_wait(barrier, 34)
+
+    def message_copy(k):
+        to = (node + k) % 32
+        return pltpu.make_async_remote_copy(
+            src_ref=outbox.at[to],
+            dst_ref=inbox.at[node],
+            send_sem=msg_send.at[k],
+            recv_sem=msg_recv.at[k],
+            device_id=(at["z"], to),
+            device_id_type=MESH,
+        )
+
+    def send_message(k, carry):
+        message_copy(k).start()
+        return carry
+
+    def wait_message(k, carry):
+        message_copy(k).wait_recv()
+        return carry
+
+    lax.fori_loop(1, 32, send_message, 0)
+    inbox[node] = outbox[node]
+    my_rows = pl.ds(pl.multiple_of(at["z"] * 32, 32), 32)
+    load_uw.wait()
+    rows_f[...] = (
+        jnp.dot(feats_ref[my_rows], uw[pl.ds(0, 1024)], preferred_element_type=F32) + ub_ref[...]
+    )
+    ids = [pair_ref[:, 0:1], pair_ref[:, 1:2]] + [neg_ref[:, k : k + 1] for k in range(15)]
+    for k, column in enumerate(ids):
+        key = (
+            ((column >> 5) & 3) * 1024 + ((column >> 7) & 1) * 512 + (column >> 8) * 32 + (column & 31)
+        )
+        keys[pl.ds(k * 64, 64)] = jnp.broadcast_to(key, (64, 128))
+    lax.fori_loop(1, 32, wait_message, 0)
+
+    got = inbox[...].reshape(512, 384)
+    got_target = got[:, 256:].astype(F32)[:, 1:2]
+    lane = lax.broadcasted_iota(jnp.int32, (512, 128), 1).astype(F32)
+    to_row = pick(got_target == lane)
+    sums = lax.dot_general(to_row, got, (((0,), (0,)), ((), ())), preferred_element_type=F32)
+    average = (sums[:, :256] / jnp.maximum(sums[:, 256:257], 1.0)).astype(BF16)
+    avg_out[...] = average.reshape(4, 32, 256)
+    copies = [
+        links.start(avg_out.at[(at["z"] + d) % 4], avg_in.at[at["z"]], ring(at, "z", d))
+        for d in (1, 2, 3)
+    ]
+    avg_in[at["z"]] = avg_out[at["z"]]
+    for copy in copies:
+        copy.wait_recv()
+    rect = rows_f[...]
+    for k in range(4):
+        rect = rect + jnp.dot(
+            avg_in[k], uw[pl.ds(1024 + k * 256, 256)], preferred_element_type=F32
+        )
+    rect = jnp.maximum(rect, 0.0)
+    scale = lax.rsqrt(jnp.mean(rect * rect, axis=1, keepdims=True) + 1e-06)
+    emb = (rect * scale).astype(BF16)
+
+    chip = {"z": at["z"], "x": at["x"], "y": at["y"]}
+    for half in range(2):
+        for t in range(4):
+            for h in range(2):
+                shared[at["z"], at["x"], at["y"], half, core * 8 + t * 2 + h] = emb[
+                    h * 16 : (h + 1) * 16, half * 512 + t * 128 : half * 512 + (t + 1) * 128
+                ]
+    mine_units = (core * 8, 8)
+    crossing = table(shared, 1 - core, mine_units, **chip)
+    keeping = table(shared, core, mine_units, **chip)
+    arrivals = [links.start(crossing, crossing, sibling)]
+    arrivals.append(links.start(keeping, keeping, sibling))
+    arrivals[0].wait_recv()
+
+    def pass_on(view, to):
+        return links.start(view, view, to)
+
+    low, high = pl.ds(0, 2), pl.ds(2, 2)
+    held = lambda p, **sel: table(shared, core, GATHER_UNITS[p], **sel)
+    first = []
+    for p in range(3):
+        a = ORDERS[p][0]
+        first.append([pass_on(held(p, **chip), ring(at, a, d)) for d in (1, 2, 3)])
+
+    def both_ways(p, axis, **sel):
+        view = held(p, **sel, **{axis: at[axis]})
+        return [pass_on(view, ring(at, axis, 1)), pass_on(view, ring(at, axis, 3))]
+
+    def forward_halves(p, axis, halved, copies, **sel):
+        me = at[axis]
+        copies[0].wait_recv()
+        left = {axis: (me + 3) % 4}
+        copies.append(pass_on(held(p, **sel, **left, **{halved: low}), ring(at, axis, 1)))
+        arrivals.append(pass_on(held(p, **sel, **left), sibling))
+        copies[1].wait_recv()
+        right = {axis: (me + 1) % 4}
+        copies.append(pass_on(held(p, **sel, **right, **{halved: high}), ring(at, axis, 3)))
+        arrivals.append(pass_on(held(p, **sel, **right), sibling))
+
+    def last_halves(p, axis, copies, **sel):
+        copies[2].wait_recv()
+        copies[3].wait_recv()
+
+    def far_view(p, axis, **sel):
+        return held(p, **sel, **{axis: (at[axis] + 2) % 4})
+
+    second = []
+    for p in range(3):
+        a, b, c = ORDERS[p]
+        for d in (1, 2, 3):
+            first[p][d - 1].wait_recv()
+        second.append(both_ways(p, b, **{c: at[c]}))
+        for d in (1, 2, 3):
+            arrivals.append(
+                pass_on(held(p, **{a: (at[a] + d) % 4, b: at[b], c: at[c]}), sibling)
+            )
+    for p in range(3):
+        a, b, c = ORDERS[p]
+        forward_halves(p, b, a, second[p], **{c: at[c]})
+    third = []
+    for p in range(3):
+        a, b, c = ORDERS[p]
+        last_halves(p, b, second[p])
+        third.append(both_ways(p, c))
+        arrivals.append(pass_on(far_view(p, b, **{c: at[c]}), sibling))
+    for p in range(3):
+        a, b, c = ORDERS[p]
+        forward_halves(p, c, a, third[p])
+    for p in range(3):
+        a, b, c = ORDERS[p]
+        last_halves(p, c, third[p])
+        arrivals.append(pass_on(far_view(p, c), sibling))
+    for copy in arrivals[1:]:
+        copy.wait_recv()
+
+    for z in range(4):
+        for half in range(2):
+            for t in range(4):
+                emb_ref[pl.ds(z * 32, 32), pl.ds(half * 512 + t * 128, 128)] = shared[
+                    z, at["x"], at["y"], half, pl.ds(core * 8 + t * 2, 2)
+                ].reshape(32, 128)
+
+    acc[...] = jnp.zeros_like(acc)
+
+    def fetch(z, carry):
+        tile_lane = lax.broadcasted_iota(jnp.int32, (1088, 128), 1) + z * 1024
+        for k in range(8):
+            onehot[:, pl.ds(k * 128, 128)] = pick(keys[...] == tile_lane + k * 128)
+        for half in range(2):
+            for pair in range(2):
+                tiles = []
+                for t in (2 * pair, 2 * pair + 1):
+                    tiles.append(
+                        jnp.concatenate(
+                            [
+                                shared[z, :, :, half, pl.ds(s * 8 + t * 2, 2)].reshape(512, 128)
+                                for s in (0, 1)
+                            ],
+                            axis=0,
+                        )
+                    )
+                cols = pl.ds(half * 512 + pair * 256, 256)
+                acc[:, cols] = acc[:, cols] + jnp.dot(
+                    onehot[...], jnp.concatenate(tiles, axis=1), preferred_element_type=F32
+                )
+        return carry
+
+    lax.fori_loop(0, 4, fetch, 0)
+    q_ref[...] = acc[pl.ds(0, 64)].astype(BF16)
+    cand_ref[...] = acc[pl.ds(64, 1024)].astype(BF16)
+    load_hw.wait()
 
     query = q_ref[...]
     q2[pl.ds(0, 64)] = query
@@ -296,20 +504,37 @@
     gw_ref[:, other_cols] = final_in[...]
     lax.fori_loop(0, 12, lambda j, carry: (core_copy(j).wait_send(), carry)[1], 0)
     links.drain()
-
-
-def score_reduce(query, cand, hidden_weight, hidden_bias, score_weight, score_grad):
+    lax.fori_loop(1, 32, lambda k, carry: (message_copy(k).wait_send(), carry)[1], 0)
+
+
+def network(*args):
     vmem = pl.BlockSpec(memory_space=pltpu.VMEM)
+    hbm = pl.BlockSpec(memory_space=pl.ANY)
     return pl.pallas_call(
-        score_kernel,
+        network_kernel,
         out_shape=(
+            jax.ShapeDtypeStruct((128, 1024), BF16),
             jax.ShapeDtypeStruct((64, 16), F32),
             jax.ShapeDtypeStruct((24, 1024), F32),
             jax.ShapeDtypeStruct((2, 1024), F32),
         ),
-        in_specs=[vmem] * 6,
-        out_specs=(vmem, vmem, vmem),
+        in_specs=[vmem, hbm] + [vmem] * 5 + [hbm] + [vmem] * 3 + [hbm] + [vmem] * 3,
+        out_specs=(vmem,) * 4,
         scratch_shapes=[
+            pltpu.VMEM((1024, 256), BF16),
+            pltpu.VMEM((2048, 1024), BF16),
+            pltpu.VMEM((3072, 1024), BF16),
+            pltpu.VMEM((32, 16, 384), BF16),
+            pltpu.VMEM((32, 16, 384), BF16),
+            pltpu.VMEM((4, 32, 256), BF16),
+            pltpu.VMEM((4, 32, 256), BF16),
+            pltpu.VMEM((32, 1024), F32),
+            pltpu.VMEM((4, 4, 4, 2, 16, 16, 128), BF16),
+            pltpu.VMEM((1088, 128), jnp.int32),
+            pltpu.VMEM((1088, 1024), BF16),
+            pltpu.VMEM((1088, 1024), F32),
+            pltpu.VMEM((64, 1024), BF16),
+            pltpu.VMEM((1024, 1024), BF16),
             pltpu.VMEM((128, 1024), BF16),
             pltpu.VMEM((128, 1024), BF16),
             pltpu.VMEM((1024, 1024), BF16),
@@ -330,24 +555,20 @@
             pltpu.VMEM((2, 1024), F32),
             pltpu.VMEM((2, 1024), F32),
             pltpu.VMEM((9, 2, 1024), F32),
+            pltpu.SemaphoreType.DMA((3,)),
+            pltpu.SemaphoreType.DMA((32,)),
+            pltpu.SemaphoreType.DMA((32,)),
             pltpu.SemaphoreType.DMA((12,)),
             pltpu.SemaphoreType.DMA((12,)),
-            pltpu.SemaphoreType.DMA((64,)),
-            pltpu.SemaphoreType.DMA((64,)),
+            pltpu.SemaphoreType.DMA((128,)),
+            pltpu.SemaphoreType.DMA((128,)),
         ],
         compiler_params=pltpu.CompilerParams(
-            collective_id=0, has_side_effects=True, vmem_limit_bytes=48 * 2**20
+            collective_id=0, has_side_effects=True, vmem_limit_bytes=60 * 2**20
         ),
-        cost_estimate=pl.CostEstimate(flops=13 * 10**9, bytes_accessed=12 * 10**6, transcendentals=10**6),
-        name="score_reduce",
-    )(
-        query,
-        cand,
-        hidden_weight,
-        hidden_bias.reshape(1, 1024),
-        score_weight.astype(F32).reshape(1, 1024),
-        score_grad,
-    )
+        cost_estimate=pl.CostEstimate(flops=22 * 10**9, bytes_accessed=14 * 10**6, transcendentals=10**6),
+        name="network",
+    )(*args)
 
 
 def body(
@@ -367,69 +588,26 @@
     score_weight,
     score_grad,
 ):
-    node_count = lax.axis_size("node")
-    node_dev, feature_dim = node_feats.shape
-    edges_dev = edge_source.shape[0]
-    slot_count = max(2, 2 * edges_dev // node_count)
-    project = jax.nn.relu(
-        jnp.dot(node_feats, msg_weight, preferred_element_type=jnp.float32) + msg_bias
-    )
-    weight_f = edge_weight.astype(jnp.float32)
-    message = (weight_f[:, None] * project[edge_source]).astype(jnp.bfloat16)
-    slot_total = node_count * slot_count
-    buffer = jnp.zeros((slot_total, feature_dim), jnp.bfloat16).at[edge_slot].set(message)
-    weight_slots = jnp.zeros((slot_total,), jnp.bfloat16).at[edge_slot].set(edge_weight)
-    target_slots = jnp.zeros((slot_total,), jnp.int32).at[edge_slot].set(edge_target)
-    got_rows, got_weights, got_targets = (
-        lax.all_to_all(
-            buffer.reshape(node_count, slot_count, feature_dim),
-            "node",
-            split_axis=0,
-            concat_axis=0,
-            tiled=True,
-        ),
-        lax.all_to_all(
-            weight_slots.reshape(node_count, slot_count),
-            "node",
-            split_axis=0,
-            concat_axis=0,
-            tiled=True,
-        ),
-        lax.all_to_all(
-            target_slots.reshape(node_count, slot_count),
-            "node",
-            split_axis=0,
-            concat_axis=0,
-            tiled=True,
-        ),
-    )
-    onehot = (
-        got_targets.reshape(-1)[None, :] == jnp.arange(node_dev, dtype=jnp.int32)[:, None]
-    ).astype(jnp.bfloat16)
-    sums = jnp.dot(onehot, got_rows.reshape(-1, feature_dim), preferred_element_type=jnp.float32)
-    totals = jnp.dot(onehot, got_weights.reshape(-1), preferred_element_type=jnp.float32)
-    average = (sums / jnp.maximum(totals, 1.0)[:, None]).astype(jnp.bfloat16)
-    joined = jnp.concatenate([node_feats, average], axis=1)
-    rectified = jax.nn.relu(
-        jnp.dot(joined, update_weight, preferred_element_type=jnp.float32) + update_bias
-    )
-    embedding = (
-        rectified * lax.rsqrt(jnp.mean(rectified * rectified, axis=-1, keepdims=True) + 1e-06)
-    ).astype(jnp.bfloat16)
-    cand_ids = jnp.concatenate([pair_ids[:, 1:2], neg_ids], axis=1).T.reshape(-1)
-    ask_ids = jnp.concatenate([pair_ids[:, 0], cand_ids])
-    shard_rows = lax.all_gather(embedding, "node", axis=0, tiled=True)
-    onehot = (ask_ids[:, None] == jnp.arange(shard_rows.shape[0], dtype=jnp.int32)[None, :]).astype(
-        jnp.bfloat16
-    )
-    fetched = jnp.dot(onehot, shard_rows, preferred_element_type=jnp.float32).astype(jnp.bfloat16)
-    scores, shared_weight, aux = score_reduce(
-        fetched[:64], fetched[64:], hidden_weight, hidden_bias, score_weight, score_grad
+    embedding, scores, shared_weight, aux = network(
+        node_feats,
+        msg_weight,
+        msg_bias.reshape(1, 1024),
+        edge_source.reshape(1, 256),
+        edge_slot.reshape(1, 256),
+        edge_target.reshape(1, 256),
+        edge_weight.astype(F32).reshape(1, 256),
+        update_weight,
+        update_bias.reshape(1, 1024),
+        pair_ids,
+        neg_ids,
+        hidden_weight,
+        hidden_bias.reshape(1, 1024),
+        score_weight.astype(F32).reshape(1, 1024),
+        score_grad,
     )
     index = lax.axis_index("pair") * 32 + lax.axis_index("node")
     mine = lax.dynamic_slice(aux, (0, index * 8), (2, 8))
-    shared_bias, shared_score = mine[0], mine[1]
-    return (embedding, scores, shared_weight, shared_bias, shared_score)
+    return (embedding, scores, shared_weight, mine[0], mine[1])
 
 
 def solution(mesh):

time: 192 us -> 126 us (0.66)
  waiting for transfers between devices: 71.6 us -> 0 us
  Pallas kernels: 53.6 us -> 113 us
  starting transfers between devices: 18.7 us -> 0 us
  matrix products: 16.8 us -> 0 us
  between operations: 14.3 us -> 0.65 us
  other arithmetic: 7.72 us -> 2.52 us
    pallas_call x1, Pallas kernels: 53.6 us -> 113 us  [network(): pl.pallas_call(network_kernel, out_shape=(jax.ShapeDtypeStruct((128, 1024...]
    all_gather x1 -> x0, waiting for transfers between devices: 51.6 us -> none  [body(): shard_rows = lax.all_gather(embedding, 'node', axis=0, tiled=True)]
    all_to_all x3 -> x0, waiting for transfers between devices: 20 us -> none  [the longest x1 15.3 us: body(): lax.all_to_all(buffer.reshape(node_count, slot_count, feature_dim), 'node...]
    all_to_all x3 -> x0, starting transfers between devices: 18.6 us -> none  [the longest x1 8.59 us: body(): lax.all_to_all(weight_slots.reshape(node_count, slot_count), 'node', spli...]
    dot_general x5 -> x0, matrix products: 16.8 us -> none  [the longest x1 11.9 us: body(): jnp.dot(onehot, shard_rows, preferred_element_type=jnp.float32)]
    unnamed x19 -> x6, local copies, waits for them, and re-layouts: 1.91 us -> 8.79 us
    scatter x1 -> x0, other arithmetic: 3.89 us -> none  [body(): jnp.zeros((slot_total, feature_dim), jnp.bfloat16).at[edge_slot]]
    scatter x2 -> x0, local copies, waits for them, and re-layouts: 3.84 us -> none  [the longest x1 2.29 us: body(): jnp.zeros((slot_total,), jnp.bfloat16).at[edge_slot].set(edge_weight)]
  transfers between devices with their start and end apart: 4 -> 0, of which waited for: 4 -> 0; matrix products, arithmetic and copies ran while one was open for 5% -> 0% of each run, Pallas kernels for 0% -> 0%
where the time goes in v2:
time: 126 us
  Pallas kernels  113 us (90%)
  local copies, waits for them, and re-layouts  10.1 us (8%)
  other arithmetic  2.52 us (2%)
    pallas_call x1, Pallas kernels, network(): pl.pallas_call(network_kernel, out_shape=(jax.ShapeDtypeStruct((128, 1024...  113 us
    unnamed x6, local copies, waits for them, and re-layouts  8.79 us

profile of v2, /device:TPU:1, one launch (start us, length us, event | category | flops | bytes accessed | tf_op | source)
XLA Modules:
  0.0 125.9 jit_solution(16621709814759721933)
XLA Ops:
  0.6 1.4 %copy.20.pair_ref = s32[64,2]{1,0:T(8,128)} copy(s32[64,2]{0,1:T(2,128)} %param.24) | data formatting | bytes 1024 | tf_op args[9]
  2.0 1.4 %copy.21.neg_ref = s32[64,15]{1,0:T(8,128)} copy(s32[64,15]{0,1:T(8,128)} %param.25) | data formatting | bytes 7680 | tf_op args[10]
  3.4 1.4 %copy.22.sg_ref = f32[64,16]{1,0:T(8,128)} copy(f32[64,16]{0,1:T(8,128)} %param.29) | data formatting | bytes 8192 | tf_op args[14]
  4.8 1.3 %reshape.50 = f32[1024]{0:T(1024)} convert(bf16[1024]{0:T(1024)(128)(2,1)} %param.28) | non-fusion elementwise | flops 1024 | bytes 6144 | tf_op jit(solution)/shard_map/reshape | solution.py:605
  6.1 1.2 reshape.48
  7.3 112.7 %network.1 = (bf16[128,1024]{1,0:T(8,128)(2,1)}, f32[64,16]{1,0:T(8,128)}, f32[24,1024]{1,0:T(8,128)}, f32[2,1024]{1,0:T(2,128)}) custom-call(bf16[128,1024]{1,0:T(8,128)(2,1)} %feats_ref.1, bf16[1024,1024]{1,0:T(8,128)(2,1)} %mw_hbm.1, f32[1,1024]{1,0:T(1,128)} %bitcast.13, s32[1,256]{1,0:T(1,128)} %bitcast.16, s32[1,256]{1,0:T(1,128)} %bitcast.17, ...), custom_call_target="tpu_custom_call" | custom-call | flops 22000001024 | bytes 14000000 | tf_op jit(solution)/shard_map/network/pallas_call | solution.py:513
  120.0 0.8 constant_dynamic-slice_fusion
  120.7 0.5 slice_bitcast_fusion
  121.3 1.4 %copy.23 = f32[64,16]{0,1:T(8,128)} copy(f32[64,16]{1,0:T(8,128)} %get-tuple-element.14) | data formatting | bytes 8192
  122.7 1.7 %copy.26 = bf16[128,1024]{1,0:T(8,128)(2,1)} copy(bf16[128,1024]{1,0:T(8,128)(2,1)} %get-tuple-element.25) | data formatting | bytes 524288
  124.4 1.5 %copy.27 = f32[24,1024]{1,0:T(8,128)} copy(f32[24,1024]{1,0:T(8,128)} %get-tuple-element.27) | data formatting | bytes 196608

commit v3 on v2

--- a/solution.py
+++ b/solution.py
@@ -43,19 +43,21 @@
 
 class Links:
     def __init__(self, send_sem, recv_sem):
-        self.send_sem, self.recv_sem, self.count, self.copies = send_sem, recv_sem, 0, []
+        self.send_sem, self.recv_sem, self.copies = send_sem, recv_sem, []
+        self.sent = self.received = 0
 
     def start(self, src, dst, to):
         copy = pltpu.make_async_remote_copy(
             src_ref=src,
             dst_ref=dst,
-            send_sem=self.send_sem.at[self.count],
-            recv_sem=self.recv_sem.at[self.count],
+            send_sem=self.send_sem.at[self.sent],
+            recv_sem=self.recv_sem.at[self.received],
             device_id=to,
             device_id_type=MESH,
         )
         copy.start()
-        self.count += 1
+        self.sent += 1
+        self.received += 1
         self.copies.append(copy)
         return copy
 
@@ -65,9 +67,13 @@
     def drain(self):
         for copy in self.copies:
             copy.wait_send()
+        self.copies, self.sent = [], 0
 
 
 def add_into(dst, *srcs):
+    if len(srcs) == 1:
+        dst[...] = dst[...] + srcs[0][...]
+        return
     total = dst[...].astype(F32)
     for src in srcs:
         total = total + src[...].astype(F32)
@@ -83,11 +89,12 @@
 
 
 def network_kernel(
-    feats_ref, mw_hbm, mb_ref, source_ref, slot_ref, target_ref, weight_ref,
-    uw_hbm, ub_ref, pair_ref, neg_ref, hw_hbm, hb_ref, sw_ref, sg_ref,
-    emb_ref, scores_ref, gw_ref, aux_out_ref,
+    feats_ref, mw_hbm, mb_ref, source_ref, slot_ref, target_ref, weights_ref,
+    uw_hbm, ub_ref, pair_ref, neg_ref, hw_hbm, hb_ref, sg_in,
+    emb_ref, scores_out, gw_ref, aux_out_ref,
+    turn, sg_ref, scores_ref,
     mw, uw, hw_ref, outbox, inbox, avg_out, avg_in, rows_f, shared, keys, onehot, acc, q_ref, cand_ref,
-    q2, gq2, prod, grad, query_act, acc_bias, acc_score,
+    q2t, qt8, gq2, query_act, acc_bias, acc_score,
     own, give, take,
     opp1, near1, opp2, near2, last3, final, final_in,
     aux, aux_core, aux_in,
@@ -122,7 +129,7 @@
         return jnp.where(cond, 1.0, 0.0).astype(BF16)
 
     row = lax.broadcasted_iota(jnp.int32, (128, 256), 0)
-    weight = weight_ref[...]
+    weight = weights_ref[:, pl.ds(1024, 256)]
     target = target_ref[...].astype(F32)
     from_node = jnp.where(row == source_ref[...], weight, 0.0)
     beside = jnp.where(row == 0, weight, jnp.where(row == 1, target, 0.0))
@@ -165,8 +172,15 @@
     rows_f[...] = (
         jnp.dot(feats_ref[my_rows], uw[pl.ds(0, 1024)], preferred_element_type=F32) + ub_ref[...]
     )
-    ids = [pair_ref[:, 0:1], pair_ref[:, 1:2]] + [neg_ref[:, k : k + 1] for k in range(15)]
-    for k, column in enumerate(ids):
+    turn[...] = jnp.zeros_like(turn)
+    turn[pl.ds(0, 2), pl.ds(0, 64)] = pair_ref[...].astype(F32)
+    turn[pl.ds(2, 15), pl.ds(0, 64)] = neg_ref[...].astype(F32)
+    turn[pl.ds(32, 16), pl.ds(0, 64)] = sg_in[...]
+    turned = turn[...].T[:64]
+    sg_ref[...] = turned[:, 32:48]
+    ids = turned[:, :17].astype(jnp.int32)
+    for k in range(17):
+        column = ids[:, k : k + 1]
         key = (
             ((column >> 5) & 3) * 1024 + ((column >> 7) & 1) * 512 + (column >> 8) * 32 + (column & 31)
         )
@@ -308,30 +322,34 @@
     cand_ref[...] = acc[pl.ds(64, 1024)].astype(BF16)
     load_hw.wait()
 
-    query = q_ref[...]
-    q2[pl.ds(0, 64)] = query
-    q2[pl.ds(64, 64)] = query
-    query_act[...] = jnp.dot(query, hw_ref[pl.ds(0, 1024)], preferred_element_type=F32) + hb_ref[...]
+    links.drain()
+    candt, prodt = uw.at[pl.ds(0, 1024)], uw.at[pl.ds(1024, 1024)]
+    grad = onehot.at[pl.ds(0, 1024)]
+    query_t = q_ref[...].T
+    q2t[...] = jnp.concatenate([query_t, query_t], axis=1)
+    qt8[...] = jnp.concatenate([query_t] * 8, axis=1)
+    query_act[...] = jnp.dot(q_ref[...], hw_ref[pl.ds(0, 1024)], preferred_element_type=F32) + hb_ref[...]
     acc_bias[...] = jnp.zeros_like(acc_bias)
     acc_score[...] = jnp.zeros_like(acc_score)
     scores_ref[...] = jnp.zeros_like(scores_ref)
 
     def forward(i, query_grad):
-        rows = pl.ds(pl.multiple_of(i * 256, 256), 256)
+        rows = pl.ds(pl.multiple_of(i * 512, 512), 512)
         cand = cand_ref[rows]
-        query = q_ref[...]
-        product = (cand.astype(F32).reshape(4, 64, 1024) * query.astype(F32)[None]).astype(BF16).reshape(256, 1024)
-        prod[rows] = product
+        product = (cand.reshape(8, 64, 1024) * q_ref[...][None]).reshape(512, 1024)
         act = jnp.dot(cand, hw_ref[pl.ds(1024, 1024)], preferred_element_type=F32)
         act = act + jnp.dot(product, hw_ref[pl.ds(2048, 1024)], preferred_element_type=F32)
-        sw = sw_ref[...].astype(F32)
+        flipped = cand.T
+        candt[:, rows] = flipped
+        prodt[:, rows] = flipped * qt8[...]
+        sw = weights_ref[:, pl.ds(0, 1024)]
         sg = sg_ref[...]
         lane = lax.broadcasted_iota(jnp.int32, (64, 16), 1)
         score = scores_ref[...]
         bias_sum = acc_bias[...]
         score_sum = acc_score[...]
-        for k in range(4):
-            mine = lane == i * 4 + k
+        for k in range(8):
+            mine = lane == i * 8 + k
             x = act[k * 64 : (k + 1) * 64] + query_act[...]
             s = 0.5 * jnp.tanh(0.5 * x) + 0.5
             hidden = (x * s).astype(BF16).astype(F32)
@@ -339,7 +357,7 @@
             cot = jnp.sum(jnp.where(mine, sg, 0.0), axis=1, keepdims=True)
             score_sum = score_sum + jnp.sum((cot * hidden).reshape(8, 8, 1024), axis=0)
             pre_grad = (cot * sw * s * (1.0 + x * (1.0 - s))).astype(BF16)
-            grad[pl.ds(pl.multiple_of(i * 256 + k * 64, 64), 64)] = pre_grad
+            grad[pl.ds(pl.multiple_of(i * 512 + k * 64, 64), 64)] = pre_grad
             pre_grad = pre_grad.astype(F32)
             bias_sum = bias_sum + jnp.sum(pre_grad.reshape(8, 8, 1024), axis=0)
             query_grad = query_grad + pre_grad
@@ -348,7 +366,7 @@
         acc_score[...] = score_sum
         return query_grad
 
-    query_grad = lax.fori_loop(0, 4, forward, jnp.zeros((64, 1024), F32))
+    query_grad = lax.fori_loop(0, 2, forward, jnp.zeros((64, 1024), F32))
     high = query_grad.astype(BF16)
     gq2[pl.ds(0, 64)] = high
     gq2[pl.ds(64, 64)] = (query_grad - high.astype(F32)).astype(BF16)
@@ -356,62 +374,61 @@
     aux[pl.ds(1, 1)] = jnp.sum(acc_score[...], axis=0, keepdims=True)
     aux_core_copy = links.start(aux, aux_core, sibling)
 
-    def core_copy(j):
-        blocks = pl.ds(j * 16, 16)
+    def core_copy(n, j):
         return pltpu.make_async_remote_copy(
-            src_ref=give.at[blocks],
-            dst_ref=take.at[blocks],
-            send_sem=core_send.at[j],
-            recv_sem=core_recv.at[j],
+            src_ref=give.at[n, j],
+            dst_ref=take.at[n, j],
+            send_sem=core_send.at[n * 6 + j],
+            recv_sem=core_recv.at[n * 6 + j],
             device_id=sibling,
             device_id_type=MESH,
         )
 
+    def chunk(n, j, xt_ref, g_ref, k):
+        x = xt_ref[pl.ds(pl.multiple_of(k * 512, 512), 512), :]
+        cols = pl.ds(pl.multiple_of((1 - core) * 512 + n * 256, 256), 256)
+        other = jnp.dot(x, g_ref[:, cols], preferred_element_type=F32)
+        give[n, j] = other.astype(BF16).reshape(32, 16, 256)
+        core_copy(n, j).start()
+        cols = pl.ds(pl.multiple_of(core * 512 + n * 256, 256), 256)
+        mine = jnp.dot(x, g_ref[:, cols], preferred_element_type=F32).astype(BF16)
+        for b in range(32):
+            own[(n,) + spot(j * 32 + b)] = mine[b * 16 : (b + 1) * 16]
+
+    def land(n, j):
+        core_copy(n, j).wait_recv()
+        for b in range(32):
+            to = (n,) + spot(j * 32 + b)
+            own[to] = own[to] + take[n, j, b]
+
+    def loop(body):
+        for k in range(2):
+            body(k)
+
+    def step_c(n):
+        def run(k):
+            chunk(n, k + 2, candt, grad, k)
+            if n == 1:
+                land(0, k)
+
+        loop(run)
+
+    def step_p(n):
+        def run(k):
+            chunk(n, k + 4, prodt, grad, k)
+            land(n, k + 2)
+
+        loop(run)
+
+    def step_q(n):
+        def run(k):
+            chunk(n, k, q2t, gq2, k)
+            land(n, k + 4)
+
+        loop(run)
+
     my_cols = pl.ds(pl.multiple_of(core * 512, 512), 512)
     other_cols = pl.ds(pl.multiple_of((1 - core) * 512, 512), 512)
-    contract = (((0,), (0,)), ((), ()))
-
-    def chunk(j, x_ref, g_ref, k):
-        x = x_ref[:, pl.ds(pl.multiple_of(k * 256, 256), 256)]
-        other = lax.dot_general(x, g_ref[:, other_cols], contract, preferred_element_type=F32)
-        give[pl.ds(j * 16, 16)] = other.astype(BF16).reshape(16, 16, 512)
-        core_copy(j).start()
-        mine = lax.dot_general(x, g_ref[:, my_cols], contract, preferred_element_type=F32)
-        mine = mine.astype(BF16)
-        for b in range(16):
-            own[spot(j * 16 + b)] = mine[b * 16 : (b + 1) * 16]
-
-    def land(j):
-        core_copy(j).wait_recv()
-        for b in range(16):
-            n = j * 16 + b
-            own[spot(n)] = (own[spot(n)].astype(F32) + take[n].astype(F32)).astype(BF16)
-
-    def weight_c(k, carry):
-        chunk(k + 4, cand_ref, grad, k)
-        return carry
-
-    def weight_p(k, carry):
-        chunk(k + 8, prod, grad, k)
-        land(k + 4)
-        return carry
-
-    def weight_q(k, carry):
-        chunk(k, q2, gq2, k)
-        land(k + 8)
-        return carry
-
-    def weight_last(k, carry):
-        land(k)
-        return carry
-
-    lax.fori_loop(0, 4, weight_c, 0)
-    lax.fori_loop(0, 4, weight_p, 0)
-    lax.fori_loop(0, 4, weight_q, 0)
-    aux_core_copy.wait()
-    links.drop(aux_core_copy)
-    add_into(aux, aux_core)
-    lax.fori_loop(0, 4, weight_last, 0)
 
     low, high_half = pl.ds(0, 2), pl.ds(2, 2)
 
@@ -452,57 +469,97 @@
             copy.wait_recv()
         add_into(view(at[axis], pl.ds(0, 4)), near.at[0], near.at[1])
 
-    def view1(third):
+    def view1(n, third):
         axis = ORDERS[third][0]
         halved = "x" if axis == "z" else "z"
-        return lambda i, h: part(own, third, **{axis: i, halved: h})
-
-    def view2(third):
+        return lambda i, h: part(own.at[n], third, **{axis: i, halved: h})
+
+    def view2(n, third):
         a, b, c = ORDERS[third]
-        return lambda i, h: part(own, third, **{a: at[a], b: i, c: h})
-
+        return lambda i, h: part(own.at[n], third, **{a: at[a], b: i, c: h})
+
+    def stage1_first(n):
+        return [first_sends(view1(n, t), opp1.at[n, t], near1.at[n, t], ORDERS[t][0]) for t in range(3)]
+
+    def stage1_second(n, copies):
+        for t in range(3):
+            second_sends(view1(n, t), opp1.at[n, t], near1.at[n, t], ORDERS[t][0], copies[t])
+
+    def stage2_first(n, copies):
+        sent = []
+        for t in range(3):
+            finish(view1(n, t), near1.at[n, t], ORDERS[t][0], copies[t])
+            sent.append(first_sends(view2(n, t), opp2.at[n, t], near2.at[n, t], ORDERS[t][1]))
+        return sent
+
+    def stage2_second(n, copies):
+        for t in range(3):
+            second_sends(view2(n, t), opp2.at[n, t], near2.at[n, t], ORDERS[t][1], copies[t])
+
+    def stage3(n, copies):
+        sent = []
+        for t in range(3):
+            finish(view2(n, t), near2.at[n, t], ORDERS[t][1], copies[t])
+            a, b, c = ORDERS[t]
+            sent.append(
+                [
+                    links.start(
+                        part(own.at[n], t, **{a: at[a], b: at[b], c: (at[c] + d) % 4}),
+                        last3.at[n, t, d - 1],
+                        ring(at, c, d),
+                    )
+                    for d in (1, 2, 3)
+                ]
+            )
+        return sent
+
+    def total(n, copies):
+        for t in range(3):
+            value = part(own.at[n], t, z=at["z"], x=at["x"], y=at["y"])[...].astype(F32)
+            for d in (1, 2, 3):
+                copies[t][d - 1].wait_recv()
+                value = value + last3[n, t, d - 1].astype(F32)
+            final[pl.ds(t * 16, 16), pl.ds(n * 256, 256)] = value
+
+    step_c(0)
+    step_p(0)
+    step_q(0)
+    step_c(1)
+    left_1 = stage1_first(0)
+    aux_core_copy.wait()
+    links.drop(aux_core_copy)
+    add_into(aux, aux_core)
     small = aux_start(0)
-    one = [first_sends(view1(t), opp1.at[t], near1.at[t], ORDERS[t][0]) for t in range(3)]
-    for t in range(3):
-        second_sends(view1(t), opp1.at[t], near1.at[t], ORDERS[t][0], one[t])
+    step_p(1)
+    stage1_second(0, left_1)
+    step_q(1)
+    left_2 = stage2_first(0, left_1)
+    loop(lambda k: land(1, k))
+    right_1 = stage1_first(1)
     aux_add(0, small)
     small = aux_start(1)
-    two = []
-    for t in range(3):
-        finish(view1(t), near1.at[t], ORDERS[t][0], one[t])
-        two.append(first_sends(view2(t), opp2.at[t], near2.at[t], ORDERS[t][1]))
-    for t in range(3):
-        second_sends(view2(t), opp2.at[t], near2.at[t], ORDERS[t][1], two[t])
+    stage2_second(0, left_2)
+    stage1_second(1, right_1)
+    left_3 = stage3(0, left_2)
+    right_2 = stage2_first(1, right_1)
     aux_add(1, small)
     small = aux_start(2)
-    three = []
-    for t in range(3):
-        finish(view2(t), near2.at[t], ORDERS[t][1], two[t])
-        a, b, c = ORDERS[t]
-        three.append(
-            [
-                links.start(
-                    part(own, t, **{a: at[a], b: at[b], c: (at[c] + d) % 4}),
-                    last3.at[t, d - 1],
-                    ring(at, c, d),
-                )
-                for d in (1, 2, 3)
-            ]
-        )
-    for t in range(3):
-        total = part(own, t, z=at["z"], x=at["x"], y=at["y"])[...].astype(F32)
-        for d in (1, 2, 3):
-            three[t][d - 1].wait_recv()
-            total = total + last3[t, d - 1].astype(F32)
-        final[pl.ds(t * 16, 16)] = total
+    stage2_second(1, right_2)
+    total(0, left_3)
+    right_3 = stage3(1, right_2)
+    total(1, right_3)
     swap = links.start(final.at[pl.ds(pl.multiple_of((1 - core) * 24, 8), 24)], final_in, sibling)
     gw_ref[:, my_cols] = final[pl.ds(pl.multiple_of(core * 24, 8), 24)]
 
     aux_add(2, small)
-    aux_out_ref[...] = aux[...]
+    index = at["z"] * 32 + node
+    near = aux[:, pl.ds(pl.multiple_of(index // 16 * 128, 128), 128)]
+    aux_out_ref[...] = pltpu.roll(near, (16 - index % 16) * 8 % 128, axis=1)
+    turn[pl.ds(0, 64), pl.ds(0, 16)] = scores_ref[...]
+    scores_out[...] = turn[...].T[:16, :64]
     swap.wait_recv()
     gw_ref[:, other_cols] = final_in[...]
-    lax.fori_loop(0, 12, lambda j, carry: (core_copy(j).wait_send(), carry)[1], 0)
+    lax.fori_loop(0, 6, lambda j, carry: (core_copy(0, j).wait_send(), core_copy(1, j).wait_send(), carry)[2], 0)
     links.drain()
     lax.fori_loop(1, 32, lambda k, carry: (message_copy(k).wait_send(), carry)[1], 0)
 
@@ -514,13 +571,16 @@
         network_kernel,
         out_shape=(
             jax.ShapeDtypeStruct((128, 1024), BF16),
-            jax.ShapeDtypeStruct((64, 16), F32),
+            jax.ShapeDtypeStruct((16, 64), F32),
             jax.ShapeDtypeStruct((24, 1024), F32),
-            jax.ShapeDtypeStruct((2, 1024), F32),
+            jax.ShapeDtypeStruct((2, 128), F32),
         ),
-        in_specs=[vmem, hbm] + [vmem] * 5 + [hbm] + [vmem] * 3 + [hbm] + [vmem] * 3,
+        in_specs=[vmem, hbm] + [vmem] * 5 + [hbm] + [vmem] * 3 + [hbm] + [vmem] * 2,
         out_specs=(vmem,) * 4,
         scratch_shapes=[
+            pltpu.VMEM((128, 128), F32),
+            pltpu.VMEM((64, 16), F32),
+            pltpu.VMEM((64, 16), F32),
             pltpu.VMEM((1024, 256), BF16),
             pltpu.VMEM((2048, 1024), BF16),
             pltpu.VMEM((3072, 1024), BF16),
@@ -535,21 +595,20 @@
             pltpu.VMEM((1088, 1024), F32),
             pltpu.VMEM((64, 1024), BF16),
             pltpu.VMEM((1024, 1024), BF16),
+            pltpu.VMEM((1024, 128), BF16),
+            pltpu.VMEM((1024, 512), BF16),
             pltpu.VMEM((128, 1024), BF16),
-            pltpu.VMEM((128, 1024), BF16),
-            pltpu.VMEM((1024, 1024), BF16),
-            pltpu.VMEM((1024, 1024), BF16),
             pltpu.VMEM((64, 1024), F32),
             pltpu.VMEM((8, 1024), F32),
             pltpu.VMEM((8, 1024), F32),
-            pltpu.VMEM((4, 4, 4, 3, 16, 512), BF16),
-            pltpu.VMEM((192, 16, 512), BF16),
-            pltpu.VMEM((192, 16, 512), BF16),
-            pltpu.VMEM((3, 2, 2, 4, 16, 512), BF16),
-            pltpu.VMEM((3, 2, 4, 4, 16, 512), BF16),
-            pltpu.VMEM((3, 2, 2, 16, 512), BF16),
-            pltpu.VMEM((3, 2, 4, 16, 512), BF16),
-            pltpu.VMEM((3, 3, 16, 512), BF16),
+            pltpu.VMEM((2, 4, 4, 4, 3, 16, 256), BF16),
+            pltpu.VMEM((2, 6, 32, 16, 256), BF16),
+            pltpu.VMEM((2, 6, 32, 16, 256), BF16),
+            pltpu.VMEM((2, 3, 2, 2, 4, 16, 256), BF16),
+            pltpu.VMEM((2, 3, 2, 4, 4, 16, 256), BF16),
+            pltpu.VMEM((2, 3, 2, 2, 16, 256), BF16),
+            pltpu.VMEM((2, 3, 2, 4, 16, 256), BF16),
+            pltpu.VMEM((2, 3, 3, 16, 256), BF16),
             pltpu.VMEM((48, 512), F32),
             pltpu.VMEM((24, 512), F32),
             pltpu.VMEM((2, 1024), F32),
@@ -560,8 +619,8 @@
             pltpu.SemaphoreType.DMA((32,)),
             pltpu.SemaphoreType.DMA((12,)),
             pltpu.SemaphoreType.DMA((12,)),
-            pltpu.SemaphoreType.DMA((128,)),
-            pltpu.SemaphoreType.DMA((128,)),
+            pltpu.SemaphoreType.DMA((104,)),
+            pltpu.SemaphoreType.DMA((176,)),
         ],
         compiler_params=pltpu.CompilerParams(
             collective_id=0, has_side_effects=True, vmem_limit_bytes=60 * 2**20
@@ -569,6 +628,32 @@
         cost_estimate=pl.CostEstimate(flops=22 * 10**9, bytes_accessed=14 * 10**6, transcendentals=10**6),
         name="network",
     )(*args)
+
+
+def hand_over_kernel(emb, scores, weight, aux, emb_out, scores_out, weight_out, bias_out, score_out):
+    emb_out[...] = emb[...]
+    scores_out[...] = scores[...]
+    weight_out[...] = weight[...]
+    bias_out[...] = aux[0:1, 0:8]
+    score_out[...] = aux[1:2, 0:8]
+
+
+def hand_over(*arrays):
+    vmem = pl.BlockSpec(memory_space=pltpu.VMEM)
+    return pl.pallas_call(
+        hand_over_kernel,
+        out_shape=(
+            jax.ShapeDtypeStruct((128, 1024), BF16),
+            jax.ShapeDtypeStruct((16, 64), F32),
+            jax.ShapeDtypeStruct((24, 1024), F32),
+            jax.ShapeDtypeStruct((1, 8), F32),
+            jax.ShapeDtypeStruct((1, 8), F32),
+        ),
+        in_specs=[vmem] * 4,
+        out_specs=(vmem,) * 5,
+        compiler_params=pltpu.CompilerParams(vmem_limit_bytes=60 * 2**20),
+        name="hand_over",
+    )(*arrays)
 
 
 def body(
@@ -588,6 +673,9 @@
     score_weight,
     score_grad,
 ):
+    weights = lax.optimization_barrier(
+        jnp.concatenate([score_weight.astype(F32), edge_weight.astype(F32)])
+    )
     embedding, scores, shared_weight, aux = network(
         node_feats,
         msg_weight,
@@ -595,19 +683,19 @@
         edge_source.reshape(1, 256),
         edge_slot.reshape(1, 256),
         edge_target.reshape(1, 256),
-        edge_weight.astype(F32).reshape(1, 256),
+        weights.reshape(1, 1280),
         update_weight,
         update_bias.reshape(1, 1024),
-        pair_ids,
-        neg_ids,
+        pair_ids.T,
+        neg_ids.T,
         hidden_weight,
         hidden_bias.reshape(1, 1024),
-        score_weight.astype(F32).reshape(1, 1024),
-        score_grad,
+        score_grad.T,
     )
-    index = lax.axis_index("pair") * 32 + lax.axis_index("node")
-    mine = lax.dynamic_slice(aux, (0, index * 8), (2, 8))
-    return (embedding, scores, shared_weight, mine[0], mine[1])
+    embedding, scores, shared_weight, shared_bias, shared_score = hand_over(
+        embedding, scores, shared_weight, aux
+    )
+    return (embedding, scores.T, shared_weight, shared_bias.reshape(8), shared_score.reshape(8))
 
 
 def solution(mesh):

time: 126 us -> 116 us (0.921)
  local copies, waits for them, and re-layouts: 10.1 us -> 0.6 us
  other arithmetic: 2.52 us -> 0.7 us
    unnamed x6 -> x0, local copies, waits for them, and re-layouts: 8.79 us -> none
    reshape x2 -> x0, other arithmetic: 2.52 us -> none  [the longest x1 1.27 us: body(): score_weight.astype(F32).reshape(1, 1024)]
    pallas_call x0 -> x1, Pallas kernels: none -> 1.74 us  [hand_over(): pl.pallas_call(hand_over_kernel, out_shape=(jax.ShapeDtypeStruct((128, 10...]
where the time goes in v3:
time: 116 us
  Pallas kernels  114 us (98%)
    pallas_call x1, Pallas kernels, network(): pl.pallas_call(network_kernel, out_shape=(jax.ShapeDtypeStruct((128, 1024...  112 us

profile of v3, /device:TPU:1, one launch (start us, length us, event | category | flops | bytes accessed | tf_op | source)
XLA Modules:
  0.0 116.2 jit_solution(8716435644724397600)
XLA Ops:
  0.6 0.7 maximum_convert_fusion
  1.3 0.6 reshape.41.weights_ref
  1.9 112.5 %network.1 = (bf16[128,1024]{1,0:T(8,128)(2,1)}, f32[16,64]{1,0:T(8,128)}, f32[24,1024]{1,0:T(8,128)}, f32[2,128]{1,0:T(2,128)}) custom-call(bf16[128,1024]{1,0:T(8,128)(2,1)} %feats_ref.1, bf16[1024,1024]{1,0:T(8,128)(2,1)} %mw_hbm.1, f32[1,1024]{1,0:T(1,128)} %bitcast.15, s32[1,256]{1,0:T(1,128)} %bitcast.18, s32[1,256]{1,0:T(1,128)} %bitcast.19, ...), custom_call_target="tpu_custom_call" | custom-call | flops 22000001024 | bytes 14000000 | tf_op jit(solution)/shard_map/network/pallas_call | solution.py:570
  114.4 1.7 %hand_over.1 = (bf16[128,1024]{1,0:T(8,128)(2,1)}, f32[16,64]{1,0:T(8,128)}, f32[24,1024]{1,0:T(8,128)}, f32[1,8]{1,0:T(1,128)}, f32[1,8]{1,0:T(1,128)}) custom-call(bf16[128,1024]{1,0:T(8,128)(2,1)} %get-tuple-element.14.emb, f32[16,64]{1,0:T(8,128)} %get-tuple-element.15.scores, f32[24,1024]{1,0:T(8,128)} %get-tuple-element.16.weight, ...), custom_call_target="tpu_custom_call" | custom-call | tf_op jit(solution)/shard_map/hand_over/pallas_call | solution.py:643

commit v4 on v3

--- a/solution.py
+++ b/solution.py
@@ -33,12 +33,14 @@
 
 def part(ref, third, **sel):
     full = pl.ds(0, 4)
-    return ref.at[sel.get("z", full), sel.get("x", full), sel.get("y", full), third]
+    a, b, c = ORDERS[third]
+    return ref.at[third, sel.get(a, full), sel.get(b, full), sel.get(c, full)]
 
 
 def spot(n):
-    chip = n // 3
-    return (chip // 16, (chip // 4) % 4, chip % 4, n % 3)
+    chip, third = n // 3, n % 3
+    at = {"z": chip // 16, "x": (chip // 4) % 4, "y": chip % 4}
+    return (third,) + tuple(at[axis] for axis in ORDERS[third])
 
 
 class Links:
@@ -93,7 +95,7 @@
     uw_hbm, ub_ref, pair_ref, neg_ref, hw_hbm, hb_ref, sg_in,
     emb_ref, scores_out, gw_ref, aux_out_ref,
     turn, sg_ref, scores_ref,
-    mw, uw, hw_ref, outbox, inbox, avg_out, avg_in, rows_f, shared, keys, onehot, acc, q_ref, cand_ref,
+    mw, uw, hw_ref, outbox, inbox, avg_out, avg_in, rows_f, shared, keys, onehot, grad, q_ref, cand_ref,
     q2t, qt8, gq2, query_act, acc_bias, acc_score,
     own, give, take,
     opp1, near1, opp2, near2, last3, final, final_in,
@@ -122,8 +124,6 @@
     load_uw = pltpu.make_async_copy(uw_hbm, uw, load_sem.at[1])
     load_hw = pltpu.make_async_copy(hw_hbm, hw_ref, load_sem.at[2])
     load_mw.start()
-    load_uw.start()
-    load_hw.start()
 
     def pick(cond):
         return jnp.where(cond, 1.0, 0.0).astype(BF16)
@@ -139,6 +139,7 @@
         to_slot, edge_rows, (((1,), (1,)), ((), ())), preferred_element_type=F32
     ).astype(BF16)
     load_mw.wait()
+    load_uw.start()
     project = jnp.dot(feats_ref[...], mw[...], preferred_element_type=F32) + mb_ref[:, quarter]
     project = jnp.maximum(project, 0.0).astype(BF16)
     message = jnp.dot(routed[:, :128], project, preferred_element_type=F32).astype(BF16)
@@ -166,6 +167,7 @@
         return carry
 
     lax.fori_loop(1, 32, send_message, 0)
+    load_hw.start()
     inbox[node] = outbox[node]
     my_rows = pl.ds(pl.multiple_of(at["z"] * 32, 32), 32)
     load_uw.wait()
@@ -234,24 +236,30 @@
         a = ORDERS[p][0]
         first.append([pass_on(held(p, **chip), ring(at, a, d)) for d in (1, 2, 3)])
 
-    def both_ways(p, axis, **sel):
-        view = held(p, **sel, **{axis: at[axis]})
-        return [pass_on(view, ring(at, axis, 1)), pass_on(view, ring(at, axis, 3))]
+    def both_ways(p, axis, halved, **sel):
+        me = {axis: at[axis]}
+        right, left = ring(at, axis, 1), ring(at, axis, 3)
+        lower = held(p, **sel, **me, **{halved: low})
+        upper = held(p, **sel, **me, **{halved: high})
+        return [pass_on(lower, right), pass_on(upper, left), pass_on(upper, right), pass_on(lower, left)]
 
     def forward_halves(p, axis, halved, copies, **sel):
-        me = at[axis]
+        left, right = {axis: (at[axis] + 3) % 4}, {axis: (at[axis] + 1) % 4}
         copies[0].wait_recv()
-        left = {axis: (me + 3) % 4}
         copies.append(pass_on(held(p, **sel, **left, **{halved: low}), ring(at, axis, 1)))
-        arrivals.append(pass_on(held(p, **sel, **left), sibling))
         copies[1].wait_recv()
-        right = {axis: (me + 1) % 4}
         copies.append(pass_on(held(p, **sel, **right, **{halved: high}), ring(at, axis, 3)))
-        arrivals.append(pass_on(held(p, **sel, **right), sibling))
+
+    def share_sides(p, axis, copies, **sel):
+        for k, step in ((2, 3), (3, 1)):
+            copies[k].wait_recv()
+            arrivals.append(
+                pass_on(held(p, **sel, **{axis: (at[axis] + step) % 4}), sibling)
+            )
 
     def last_halves(p, axis, copies, **sel):
-        copies[2].wait_recv()
-        copies[3].wait_recv()
+        copies[4].wait_recv()
+        copies[5].wait_recv()
 
     def far_view(p, axis, **sel):
         return held(p, **sel, **{axis: (at[axis] + 2) % 4})
@@ -261,7 +269,7 @@
         a, b, c = ORDERS[p]
         for d in (1, 2, 3):
             first[p][d - 1].wait_recv()
-        second.append(both_ways(p, b, **{c: at[c]}))
+        second.append(both_ways(p, b, a, **{c: at[c]}))
         for d in (1, 2, 3):
             arrivals.append(
                 pass_on(held(p, **{a: (at[a] + d) % 4, b: at[b], c: at[c]}), sibling)
@@ -269,15 +277,28 @@
     for p in range(3):
         a, b, c = ORDERS[p]
         forward_halves(p, b, a, second[p], **{c: at[c]})
+    for p in range(3):
+        a, b, c = ORDERS[p]
+        share_sides(p, b, second[p], **{c: at[c]})
     third = []
     for p in range(3):
         a, b, c = ORDERS[p]
         last_halves(p, b, second[p])
-        third.append(both_ways(p, c))
+        third.append(both_ways(p, c, a))
         arrivals.append(pass_on(far_view(p, b, **{c: at[c]}), sibling))
+    def pick_rows(k, carry):
+        start = pl.multiple_of(k * 128, 128)
+        lanes = lax.broadcasted_iota(jnp.int32, (1088, 128), 1) + start
+        onehot[:, pl.ds(start, 128)] = pick(keys[...] == lanes)
+        return carry
+
+    lax.fori_loop(0, 32, pick_rows, 0)
     for p in range(3):
         a, b, c = ORDERS[p]
         forward_halves(p, c, a, third[p])
+    for p in range(3):
+        a, b, c = ORDERS[p]
+        share_sides(p, c, third[p])
     for p in range(3):
         a, b, c = ORDERS[p]
         last_halves(p, c, third[p])
@@ -292,39 +313,33 @@
                     z, at["x"], at["y"], half, pl.ds(core * 8 + t * 2, 2)
                 ].reshape(32, 128)
 
-    acc[...] = jnp.zeros_like(acc)
-
-    def fetch(z, carry):
-        tile_lane = lax.broadcasted_iota(jnp.int32, (1088, 128), 1) + z * 1024
-        for k in range(8):
-            onehot[:, pl.ds(k * 128, 128)] = pick(keys[...] == tile_lane + k * 128)
-        for half in range(2):
-            for pair in range(2):
-                tiles = []
-                for t in (2 * pair, 2 * pair + 1):
-                    tiles.append(
-                        jnp.concatenate(
-                            [
-                                shared[z, :, :, half, pl.ds(s * 8 + t * 2, 2)].reshape(512, 128)
-                                for s in (0, 1)
-                            ],
-                            axis=0,
-                        )
-                    )
-                cols = pl.ds(half * 512 + pair * 256, 256)
-                acc[:, cols] = acc[:, cols] + jnp.dot(
-                    onehot[...], jnp.concatenate(tiles, axis=1), preferred_element_type=F32
+    def fetch(n, carry):
+        half, pair = n // 2, n % 2
+        tiles = []
+        for t in range(2):
+            tiles.append(
+                jnp.concatenate(
+                    [
+                        shared[z, :, :, half, pl.ds(s * 8 + pair * 4 + t * 2, 2)].reshape(512, 128)
+                        for z in range(4)
+                        for s in (0, 1)
+                    ],
+                    axis=0,
                 )
+            )
+        cols = pl.ds(pl.multiple_of(n * 256, 256), 256)
+        rows = jnp.dot(
+            onehot[...], jnp.concatenate(tiles, axis=1), preferred_element_type=F32
+        ).astype(BF16)
+        q_ref[:, cols] = rows[:64]
+        cand_ref[:, cols] = rows[64:]
         return carry
 
     lax.fori_loop(0, 4, fetch, 0)
-    q_ref[...] = acc[pl.ds(0, 64)].astype(BF16)
-    cand_ref[...] = acc[pl.ds(64, 1024)].astype(BF16)
     load_hw.wait()
 
     links.drain()
     candt, prodt = uw.at[pl.ds(0, 1024)], uw.at[pl.ds(1024, 1024)]
-    grad = onehot.at[pl.ds(0, 1024)]
     query_t = q_ref[...].T
     q2t[...] = jnp.concatenate([query_t, query_t], axis=1)
     qt8[...] = jnp.concatenate([query_t] * 8, axis=1)
@@ -470,9 +485,8 @@
         add_into(view(at[axis], pl.ds(0, 4)), near.at[0], near.at[1])
 
     def view1(n, third):
-        axis = ORDERS[third][0]
-        halved = "x" if axis == "z" else "z"
-        return lambda i, h: part(own.at[n], third, **{axis: i, halved: h})
+        a, b, _ = ORDERS[third]
+        return lambda i, h: part(own.at[n], third, **{a: i, b: h})
 
     def view2(n, third):
         a, b, c = ORDERS[third]
@@ -591,8 +605,8 @@
             pltpu.VMEM((32, 1024), F32),
             pltpu.VMEM((4, 4, 4, 2, 16, 16, 128), BF16),
             pltpu.VMEM((1088, 128), jnp.int32),
-            pltpu.VMEM((1088, 1024), BF16),
-            pltpu.VMEM((1088, 1024), F32),
+            pltpu.VMEM((1088, 4096), BF16),
+            pltpu.VMEM((1024, 1024), BF16),
             pltpu.VMEM((64, 1024), BF16),
             pltpu.VMEM((1024, 1024), BF16),
             pltpu.VMEM((1024, 128), BF16),
@@ -601,7 +615,7 @@
             pltpu.VMEM((64, 1024), F32),
             pltpu.VMEM((8, 1024), F32),
             pltpu.VMEM((8, 1024), F32),
-            pltpu.VMEM((2, 4, 4, 4, 3, 16, 256), BF16),
+            pltpu.VMEM((2, 3, 4, 4, 4, 16, 256), BF16),
             pltpu.VMEM((2, 6, 32, 16, 256), BF16),
             pltpu.VMEM((2, 6, 32, 16, 256), BF16),
             pltpu.VMEM((2, 3, 2, 2, 4, 16, 256), BF16),
@@ -620,7 +634,7 @@
             pltpu.SemaphoreType.DMA((12,)),
             pltpu.SemaphoreType.DMA((12,)),
             pltpu.SemaphoreType.DMA((104,)),
-            pltpu.SemaphoreType.DMA((176,)),
+            pltpu.SemaphoreType.DMA((192,)),
         ],
         compiler_params=pltpu.CompilerParams(
             collective_id=0, has_side_effects=True, vmem_limit_bytes=60 * 2**20

time: 116 us -> 114 us (0.983)
  Pallas kernels: 114 us -> 112 us
    pallas_call x1, Pallas kernels: 112 us -> 110 us  [network(): pl.pallas_call(network_kernel, out_shape=(jax.ShapeDtypeStruct((128, 1024...]
where the time goes in v4:
time: 114 us
  Pallas kernels  112 us (98%)
    pallas_call x1, Pallas kernels, network(): pl.pallas_call(network_kernel, out_shape=(jax.ShapeDtypeStruct((128, 1024...  110 us

profile of v4, /device:TPU:1, one launch (start us, length us, event | category | flops | bytes accessed | tf_op | source)
XLA Modules:
  0.0 113.5 jit_solution(11203488656122056687)
XLA Ops:
  0.6 0.7 maximum_convert_fusion
  1.3 0.6 reshape.41.weights_ref
  1.9 109.9 %network.1 = (bf16[128,1024]{1,0:T(8,128)(2,1)}, f32[16,64]{1,0:T(8,128)}, f32[24,1024]{1,0:T(8,128)}, f32[2,128]{1,0:T(2,128)}) custom-call(bf16[128,1024]{1,0:T(8,128)(2,1)} %feats_ref.1, bf16[1024,1024]{1,0:T(8,128)(2,1)} %mw_hbm.1, f32[1,1024]{1,0:T(1,128)} %bitcast.15, s32[1,256]{1,0:T(1,128)} %bitcast.18, s32[1,256]{1,0:T(1,128)} %bitcast.19, ...), custom_call_target="tpu_custom_call" | custom-call | flops 22000001024 | bytes 14000000 | tf_op jit(solution)/shard_map/network/pallas_call | solution.py:584
  111.8 1.7 %hand_over.1 = (bf16[128,1024]{1,0:T(8,128)(2,1)}, f32[16,64]{1,0:T(8,128)}, f32[24,1024]{1,0:T(8,128)}, f32[1,8]{1,0:T(1,128)}, f32[1,8]{1,0:T(1,128)}) custom-call(bf16[128,1024]{1,0:T(8,128)(2,1)} %get-tuple-element.14.emb, f32[16,64]{1,0:T(8,128)} %get-tuple-element.15.scores, f32[24,1024]{1,0:T(8,128)} %get-tuple-element.16.weight, ...), custom_call_target="tpu_custom_call" | custom-call | tf_op jit(solution)/shard_map/hand_over/pallas_call | solution.py:657
